TPU v7x, 512 devices: a whole 4x8x8 slice. The times are simulated.
512 devices in a mesh: lat: 16 (over z_hi, x, core), lon: 32 (over y, z_lo).
Axes of the slice: x: 4, y: 8, z: 8 (z_hi: 2, z_lo: 4; z = z_hi * 4 + z_lo), core: 2. Of those that a mesh axis runs over, the one named last changes fastest.
Arguments:
- tokens: bfloat16 [4, 96, 384, 512], P(None, 'lat', 'lon'), may hold values from -6 to 6
- cotangent: bfloat16 [4, 96, 384, 512], P(None, 'lat', 'lon'), may hold values from -6 to 6
- w_qkv: bfloat16 [512, 1536], replicated, may hold values from -1.06066017 to 1.06066017
- w_out: bfloat16 [512, 512], replicated, may hold values from -1 to 1
- land_mask: int32 [96, 384], replicated, may hold values 0 or 1
- land_bias: float32 [8], replicated, may hold values from -2 to 2
Outputs:
- attended: bfloat16 [4, 96, 384, 512], P(None, 'lat', 'lon')
- grad_tokens: bfloat16 [4, 96, 384, 512], P(None, 'lat', 'lon')
- grad_qkv: float32 [512, 1536], P('lat', 'lon')
- grad_out: float32 [512, 512], P('lat', 'lon')
- grad_bias: float32 [8], replicated
All inputs are finite; a program needn't handle non-finite values.
Results may differ from a plain program's by a relative error of at most 0.034.
The roundings to bfloat16 on the way count: a program that leaves them out, or rounds other values in their place, can miss the bound.
Values may be sent and summed in bfloat16 or wider, within the bound.
A program may use at most 64 MiB of HBM per device.

v0:
```python
import jax
import jax.numpy as jnp
from jax import lax
from jax.sharding import PartitionSpec as P

WLAT = 6
WLON = 12


def passed_along(block, axis, distance):
    devices = range(lax.axis_size(axis))
    route = [((i - distance) % len(devices), i) for i in devices]
    return lax.ppermute(block, axis, route)


def layer_norm(tokens_f):
    mean_value = jnp.mean(tokens_f, axis=-1, keepdims=True)
    centred = tokens_f - mean_value
    variance = jnp.mean(centred * centred, axis=-1, keepdims=True)
    inv_scale = lax.rsqrt(variance + 1e-05)
    return (centred * inv_scale, inv_scale)


def window_split(grid):
    level_count, lat_rows, lon_cols, features = grid.shape
    grid = grid.reshape(
        level_count // 2, 2, lat_rows // WLAT, WLAT, lon_cols // WLON, WLON, features
    )
    grid = grid.transpose(0, 2, 4, 1, 3, 5, 6)
    return grid.reshape(-1, 2 * WLAT * WLON, features)


def window_merge(windows, level_count, lat_rows, lon_cols):
    features = windows.shape[-1]
    grid = windows.reshape(
        level_count // 2, lat_rows // WLAT, lon_cols // WLON, 2, WLAT, WLON, features
    )
    grid = grid.transpose(0, 3, 1, 4, 2, 5, 6)
    return grid.reshape(level_count, lat_rows, lon_cols, features)


def window_attention(qkv, land, region, land_bias):
    block_count, win_len = (qkv.shape[0], qkv.shape[1])
    head_count = land_bias.shape[0]
    head_size = qkv.shape[2] // (3 * head_count)
    split_qkv = qkv.reshape(block_count, win_len, 3, head_count, head_size)
    queries = split_qkv[:, :, 0].astype(jnp.float32)
    key_vecs = split_qkv[:, :, 1].astype(jnp.float32)
    values_f = split_qkv[:, :, 2].astype(jnp.float32)
    scores = jnp.einsum("bqhd,bkhd->bhqk", queries, key_vecs) * head_size ** (-0.5)
    scores = scores + land_bias[None, :, None, None] * land.astype(jnp.float32)[:, None, None, :]
    same_region = region[:, :, None] == region[:, None, :]
    scores = jnp.where(same_region[:, None], scores, -1e30)
    peak_score = jnp.max(scores, axis=-1, keepdims=True)
    expo = jnp.exp(scores - peak_score)
    weights_bf = (expo / jnp.sum(expo, axis=-1, keepdims=True)).astype(jnp.bfloat16)
    mixed = jnp.einsum("bhqk,bkhd->bqhd", weights_bf.astype(jnp.float32), values_f)
    return mixed.reshape(block_count, win_len, head_count * head_size).astype(jnp.bfloat16)


def window_pass(tokens, grad_in, land, region, w_qkv, w_out, land_bias):
    block_count, win_len, features = tokens.shape
    normal, inv_scale = layer_norm(tokens.astype(jnp.float32))
    flat_normed = normal.astype(jnp.bfloat16).reshape(block_count * win_len, features)
    qkv = jnp.dot(flat_normed, w_qkv, preferred_element_type=jnp.float32).astype(jnp.bfloat16)
    qkv = qkv.reshape(block_count, win_len, 3 * features)

    def attend(qkv_in, bias_in):
        return window_attention(qkv_in, land, region, bias_in)

    mixed, pullback = jax.vjp(attend, qkv, land_bias)
    mixed_flat = mixed.reshape(block_count * win_len, features)
    attended = jnp.dot(mixed_flat, w_out, preferred_element_type=jnp.float32).astype(jnp.bfloat16)
    grad_flat = grad_in.reshape(block_count * win_len, features)
    d_mixed = jnp.dot(grad_flat, w_out.T, preferred_element_type=jnp.float32).astype(jnp.bfloat16)
    d_wout = jnp.dot(mixed_flat.T, grad_flat, preferred_element_type=jnp.float32)
    d_qkv, d_bias = pullback(d_mixed.reshape(block_count, win_len, features))
    d_qkv_flat = d_qkv.reshape(block_count * win_len, 3 * features)
    d_wqkv = jnp.dot(flat_normed.T, d_qkv_flat, preferred_element_type=jnp.float32)
    d_normed = jnp.dot(d_qkv_flat, w_qkv.T, preferred_element_type=jnp.float32)
    d_normed = d_normed.reshape(block_count, win_len, features)
    mean_grad = jnp.mean(d_normed, axis=-1, keepdims=True)
    mean_cross = jnp.mean(d_normed * normal, axis=-1, keepdims=True)
    d_tokens = (inv_scale * (d_normed - mean_grad - normal * mean_cross)).astype(jnp.bfloat16)
    return (attended.reshape(block_count, win_len, features), d_tokens, d_wqkv, d_wout, d_bias)


def shards(tokens, cotangent, w_qkv, w_out, land_mask, land_bias):
    level_count, lat_rows, lon_cols, features = tokens.shape
    half_lat = WLAT // 2
    half_lon = WLON // 2
    below = passed_along((tokens[:, :half_lat], cotangent[:, :half_lat]), "lat", -1)
    ext_tokens = jnp.concatenate([tokens[:, half_lat:], below[0]], axis=1)
    ext_cot = jnp.concatenate([cotangent[:, half_lat:], below[1]], axis=1)
    beside = passed_along((ext_tokens[:, :, :half_lon], ext_cot[:, :, :half_lon]), "lon", -1)
    moved_tokens = jnp.roll(
        jnp.concatenate([ext_tokens[:, :, half_lon:], beside[0]], axis=2), -1, axis=0
    )
    moved_cot = jnp.roll(jnp.concatenate([ext_cot[:, :, half_lon:], beside[1]], axis=2), -1, axis=0)
    lat_index = lax.axis_index("lat")
    lon_index = lax.axis_index("lon")
    total_rows = lat_rows * lax.axis_size("lat")
    tiled = jnp.tile(land_mask, (2, 2))
    land_local = lax.dynamic_slice(
        tiled,
        (lat_index * lat_rows + half_lat, lon_index * lon_cols + half_lon),
        (lat_rows, lon_cols),
    )
    land_grid = jnp.broadcast_to(land_local[None, :, :, None], (level_count, lat_rows, lon_cols, 1))
    global_rows = lat_index * lat_rows + jnp.arange(lat_rows)
    lat_flag = (global_rows >= total_rows - half_lat).astype(jnp.int32)
    level_flag = (jnp.arange(level_count) == level_count - 1).astype(jnp.int32)
    region_grid = (
        2 * lat_flag[None, :, None]
        + level_flag[:, None, None]
        + jnp.zeros((level_count, lat_rows, lon_cols), jnp.int32)
    )
    attended_w, d_tokens_w, d_wqkv, d_wout, d_bias = window_pass(
        window_split(moved_tokens),
        window_split(moved_cot),
        window_split(land_grid)[..., 0],
        window_split(region_grid[..., None])[..., 0],
        w_qkv,
        w_out,
        land_bias,
    )
    back_out = jnp.roll(window_merge(attended_w, level_count, lat_rows, lon_cols), 1, axis=0)
    back_grad = jnp.roll(window_merge(d_tokens_w, level_count, lat_rows, lon_cols), 1, axis=0)
    right_side = passed_along((back_out[:, :, -half_lon:], back_grad[:, :, -half_lon:]), "lon", 1)
    col_out = jnp.concatenate([right_side[0], back_out[:, :, :-half_lon]], axis=2)
    col_grad = jnp.concatenate([right_side[1], back_grad[:, :, :-half_lon]], axis=2)
    upper = passed_along((col_out[:, -half_lat:], col_grad[:, -half_lat:]), "lat", 1)
    attended = jnp.concatenate([upper[0], col_out[:, :-half_lat]], axis=1)
    grad_tokens = jnp.concatenate([upper[1], col_grad[:, :-half_lat]], axis=1)
    partial_grads = (
        lax.psum_scatter(
            d_wqkv.astype(jnp.bfloat16), "lat", scatter_dimension=0, tiled=True
        ).astype(jnp.float32),
        lax.psum_scatter(
            d_wout.astype(jnp.bfloat16), "lat", scatter_dimension=0, tiled=True
        ).astype(jnp.float32),
    )
    final_grads = (
        lax.psum_scatter(
            partial_grads[0].astype(jnp.bfloat16), "lon", scatter_dimension=1, tiled=True
        ).astype(jnp.float32),
        lax.psum_scatter(
            partial_grads[1].astype(jnp.bfloat16), "lon", scatter_dimension=1, tiled=True
        ).astype(jnp.float32),
    )
    grad_bias = lax.psum(d_bias, ("lat", "lon"))
    return (attended, grad_tokens, final_grads[0], final_grads[1], grad_bias)


def solution(mesh):
    in_specs = (P(None, "lat", "lon", None), P(None, "lat", "lon", None), P(), P(), P(), P())
    out_specs = (
        P(None, "lat", "lon", None),
        P(None, "lat", "lon", None),
        P("lat", "lon"),
        P("lat", "lon"),
        P(),
    )
    return jax.shard_map(shards, mesh=mesh, in_specs=in_specs, out_specs=out_specs, check_vma=False)
```

profile of v0, /device:TPU:6, one launch (start us, length us, event | category | flops | bytes accessed | tf_op | source)
XLA Modules:
  0.0 580.0 jit_solution(9448699388386415433)
XLA Ops:
  7.2 1.2 fusion.56
  8.4 2.2 collective-permute-start
  10.6 1.1 fusion.54
  11.7 2.6 collective-permute-start.4
  14.6 1.1 tile.4
  16.8 10.8 %collective-permute-start.1 = (bf16[4,6,6,512]{3,0,2,1:T(4,128)(2,1)S(1)}, bf16[4,6,6,512]{3,0,2,1:T(4,128)(2,1)S(1)}, u32[]{:S(2)}, u32[]{:S(2)}) collective-permute-start(bf16[4,6,6,512]{3,0,2,1:T(4,128)(2,1)S(1)} %get-tuple-element.47), channel_id=1, source_target_pairs={{1,0},{2,1},{3,2},{4,3},{5,4},{6,5},{7,6},{8,7},{9,8},{10,9},{11,1... | collective-permute-start | bytes 442376 | tf_op jit(solution)/shard_map/ppermute | solution.py:13
  28.3 0.9 fusion.41
  29.2 1.9 collective-permute-start.5
  32.0 1.0 multiply_reduce_fusion.1
  33.8 1.4 add_rsqrt_fusion
  35.2 0.9 copy.78
  36.8 1.8 multiply_convert_fusion
  40.0 1.1 reshape_reshape_transpose_reshape.3
  42.4 1.2 copy.88
  43.7 1.6 convolution_convert_fusion.1
  45.3 2.6 reshape_reshape.3
  47.9 1.3 fusion.52
  49.2 1.5 copy.109
  50.7 1.4 copy.110
  52.2 1.2 copy.111
  53.4 1.9 fusion.57
  55.7 2.7 convert_reduce_fusion
  58.5 2.3 fusion.49
  60.8 1.3 fusion.18
  64.0 1.3 convolution_convert_fusion.3
  66.3 2.7 fusion.22
  70.1 1.5 pad_add_fusion
  71.6 2.9 copy.93
  74.5 1.9 reshape.227
  76.4 3.4 convolution_convert_fusion
  80.0 2.0 reshape.229
  82.1 1.9 dot_general.47
  83.9 2.2 fusion.48
  87.3 3.9 collective-permute-start.6
  91.3 2.4 fusion.27
  94.6 1.9 collective-permute-start.2
  96.5 2.6 collective-permute-done.6
  99.1 1.1 fusion.34
  100.2 7.9 %collective-permute-start.7 = (bf16[4,3,12,512]{3,2,1,0:T(8,128)(2,1)S(1)}, bf16[4,3,12,512]{3,2,1,0:T(8,128)(2,1)S(1)}, u32[]{:S(2)}, u32[]{:S(2)}) collective-permute-start(bf16[4,3,12,512]{3,2,1,0:T(8,128)(2,1)S(1)} %get-tuple-element.38), channel_id=1, source_target_pairs={{480,0},{0,32},{32,64},{64,96},{96,128},{128,160},{160,192},{192,2... | collective-permute-start | bytes 442376 | tf_op jit(solution)/shard_map/ppermute | solution.py:13
  108.5 3.9 collective-permute-start.3
  112.4 45.6 %reduce-scatter.11.cloned.1.call-done = bf16[32,512]{1,0:T(8,128)(2,1)} async-done(((bf16[512,512]{1,0:T(8,128)(2,1)}), bf16[32,512]{1,0:T(8,128)(2,1)}) %reduce-scatter.11.cloned.1.call-update) | async-done | bytes 32784 | tf_op jit(solution)/shard_map/reduce_scatter | solution.py:139
  158.0 1.5 copy.107
  159.7 95.9 %psum.7 = f32[8]{0:T(128)} all-reduce(f32[8]{0:T(128)S(1)} %multiply_reduce_fusion.2), channel_id=1, replica_groups=mesh['lat'=16,'lon'=32] {'lat','lon'}, use_global_device_ids=true, to_apply=%region_15.16 | all-reduce | flops 8 | bytes 64 | tf_op jit(solution)/shard_map/psum | solution.py:151
  255.6 1.8 copy.105
  257.5 0.9 copy.99
  258.5 0.9 pad_maximum_fusion.5
  259.4 152.0 %reduce-scatter.15.cloned.1.call-done = bf16[16,32]{1,0:T(8,128)(2,1)} async-done(((bf16[512,32]{1,0:T(8,128)(2,1)}), bf16[16,32]{1,0:T(8,128)(2,1)}) %reduce-scatter.15.cloned.1.call-update) | async-done | bytes 1040
  412.8 159.3 %reduce-scatter.13.cloned.1.call-done = bf16[48,32]{1,0:T(8,128)(2,1)} async-done(((bf16[1536,32]{1,0:T(8,128)(2,1)}), bf16[48,32]{1,0:T(8,128)(2,1)}) %reduce-scatter.13.cloned.1.call-update) | async-done | bytes 3088
  (127 shorter events, 17.2 us)
Async XLA Ops:
  7.2 36.5 %copy-start = (bf16[512,1536]{1,0:T(8,128)(2,1)S(1)}, bf16[512,1536]{1,0:T(8,128)(2,1)}, u32[]{:S(2)}) copy-start(bf16[512,1536]{1,0:T(8,128)(2,1)} %param.8) | copy-start | bytes 4718596
  7.2 20.5 %copy-start.25 = (f32[8]{0:T(128)S(1)}, f32[8]{0:T(128)}, u32[]{:S(2)}) copy-start(f32[8]{0:T(128)} %param.11) | copy-start | bytes 100
  7.2 150.8 %reduce-scatter.11.cloned.1.call-start = ((), (), s32[]{:S(2)}) async-start(), calls=%async_computation.5 | async-start | bytes 557056 | tf_op jit(solution)/shard_map/reduce_scatter | solution.py:139
  8.4 8.2 %collective-permute-start = (bf16[4,3,12,512]{3,0,2,1:T(4,128)(2,1)S(1)}, bf16[4,3,12,512]{3,0,2,1:T(4,128)(2,1)S(1)}, u32[]{:S(2)}, u32[]{:S(2)}) collective-permute-start(bf16[4,3,12,512]{3,0,2,1:T(4,128)(2,1)S(1)} %get-tuple-element.49), channel_id=1, source_target_pairs={{32,0},{64,32},{96,64},{128,96},{160,128},{192,160},{224,192},{256... | collective-permute-start | bytes 442376 | tf_op jit(solution)/shard_map/ppermute | solution.py:13
  11.7 16.6 %collective-permute-start.4 = (bf16[4,3,12,512]{3,0,2,1:T(4,128)(2,1)S(1)}, bf16[4,3,12,512]{3,0,2,1:T(4,128)(2,1)S(1)}, u32[]{:S(2)}, u32[]{:S(2)}) collective-permute-start(bf16[4,3,12,512]{3,0,2,1:T(4,128)(2,1)S(1)} %get-tuple-element.43), channel_id=1, source_target_pairs={{32,0},{64,32},{96,64},{128,96},{160,128},{192,160},{224,192},{256... | collective-permute-start | bytes 442376 | tf_op jit(solution)/shard_map/ppermute | solution.py:13
  15.9 16.1 %copy-start.20 = (f32[2,144]{1,0:T(2,128)}, f32[2,144]{1,0:T(2,128)S(1)}, u32[]{:S(2)}) copy-start(f32[2,144]{1,0:T(2,128)S(1)} %convert_element_type.140) | copy-start | bytes 3460
  16.8 14.3 %collective-permute-start.1 = (bf16[4,6,6,512]{3,0,2,1:T(4,128)(2,1)S(1)}, bf16[4,6,6,512]{3,0,2,1:T(4,128)(2,1)S(1)}, u32[]{:S(2)}, u32[]{:S(2)}) collective-permute-start(bf16[4,6,6,512]{3,0,2,1:T(4,128)(2,1)S(1)} %get-tuple-element.47), channel_id=1, source_target_pairs={{1,0},{2,1},{3,2},{4,3},{5,4},{6,5},{7,6},{8,7},{9,8},{10,9},{11,1... | collective-permute-start | bytes 442376 | tf_op jit(solution)/shard_map/ppermute | solution.py:13
  29.2 9.4 %collective-permute-start.5 = (bf16[4,6,6,512]{3,0,2,1:T(4,128)(2,1)}, bf16[4,6,6,512]{3,0,2,1:T(4,128)(2,1)S(1)}, u32[]{:S(2)}, u32[]{:S(2)}) collective-permute-start(bf16[4,6,6,512]{3,0,2,1:T(4,128)(2,1)} %get-tuple-element.41), channel_id=1, source_target_pairs={{1,0},{2,1},{3,2},{4,3},{5,4},{6,5},{7,6},{8,7},{9,8},{10,9},{11,1... | collective-permute-start | bytes 442376 | tf_op jit(solution)/shard_map/ppermute | solution.py:13
  33.0 8.8 %copy-start.6 = (bf16[512,512]{1,0:T(8,128)(2,1)S(1)}, bf16[512,512]{1,0:T(8,128)(2,1)}, u32[]{:S(2)}) copy-start(bf16[512,512]{1,0:T(8,128)(2,1)} %param.9) | copy-start | bytes 1572868
  33.1 10.6 %copy-start.2 = (f32[4,6,12,512]{3,2,1,0:T(8,128)}, f32[4,6,12,512]{3,2,1,0:T(8,128)S(1)}, u32[]{:S(2)}) copy-start(f32[4,6,12,512]{3,2,1,0:T(8,128)S(1)} %copy.73) | copy-start | bytes 1769476
  41.0 0.7 copy-start.12
  41.7 2.0 copy-start.23
  41.7 2.0 copy-start.24
  49.2 2.9 copy-start.3
  49.2 4.1 copy-start.18
  49.2 4.1 copy-start.22
  52.1 3.2 copy-start.16
  53.4 2.4 copy-start.5
  60.8 1.6 copy-start.11
  62.1 1.9 copy-start.13
  63.6 2.6 copy-start.14
  64.0 5.0 copy-start.9
  65.3 190.3 %reduce-scatter.9.cloned.1.call-start = ((), (), s32[]{:S(2)}) async-start(), calls=%async_computation.4 | async-start | bytes 1671168 | tf_op jit(solution)/shard_map/reduce_scatter | solution.py:136
  66.3 2.8 copy-start.1
  66.3 2.8 copy-start.17
  66.3 2.8 copy-start.19
  69.0 1.0 copy-start.8
  79.8 331.6 %reduce-scatter.15.cloned.1.call-start = ((), (), s32[]{:S(2)}) async-start(), calls=%async_computation.7 | async-start | bytes 135168
  83.9 2.3 copy-start.4
  86.2 5.1 copy-start.15
  86.5 7.2 %copy-start.7 = (bf16[512,512]{1,0:T(8,128)(2,1)S(1)}, bf16[512,512]{1,0:T(8,128)(2,1)}, u32[]{:S(2)}) copy-start(bf16[512,512]{1,0:T(8,128)(2,1)} %param.9) | copy-start | bytes 1572868
  86.5 7.2 %copy-start.10 = (bf16[288,512]{1,0:T(8,128)(2,1)S(1)}, bf16[288,512]{1,0:T(8,128)(2,1)}, u32[]{:S(2)}) copy-start(bf16[288,512]{1,0:T(8,128)(2,1)} %copy-done.9) | copy-start | bytes 884740
  87.3 11.8 %collective-permute-start.6 = (bf16[4,6,6,512]{3,2,1,0:T(8,128)(2,1)}, bf16[4,6,6,512]{3,2,1,0:T(8,128)(2,1)}, u32[]{:S(2)}, u32[]{:S(2)}) collective-permute-start(bf16[4,6,6,512]{3,2,1,0:T(8,128)(2,1)} %fusion.40), channel_id=1, source_target_pairs={{31,0},{0,1},{1,2},{2,3},{3,4},{4,5},{5,6},{6,7},{7,8},{8,9},{9,10... | collective-permute-start | bytes 442376 | tf_op jit(solution)/shard_map/ppermute | solution.py:13
  94.2 65.4 %copy-start.21 = (f32[2,144]{1,0:T(2,128)S(1)}, f32[2,144]{1,0:T(2,128)}, u32[]{:S(2)}) copy-start(f32[2,144]{1,0:T(2,128)} %copy-done.20) | copy-start | bytes 3460
  94.6 13.6 %collective-permute-start.2 = (bf16[4,6,6,512]{3,0,2,1:T(4,128)(2,1)S(1)}, bf16[4,6,6,512]{3,0,2,1:T(4,128)(2,1)S(1)}, u32[]{:S(2)}, u32[]{:S(2)}) collective-permute-start(bf16[4,6,6,512]{3,0,2,1:T(4,128)(2,1)S(1)} %fusion.42), channel_id=1, source_target_pairs={{31,0},{0,1},{1,2},{2,3},{3,4},{4,5},{5,6},{6,7},{7,8},{8,9},{9,10... | collective-permute-start | bytes 442376 | tf_op jit(solution)/shard_map/ppermute | solution.py:13
  100.2 157.2 %collective-permute-start.7 = (bf16[4,3,12,512]{3,2,1,0:T(8,128)(2,1)S(1)}, bf16[4,3,12,512]{3,2,1,0:T(8,128)(2,1)S(1)}, u32[]{:S(2)}, u32[]{:S(2)}) collective-permute-start(bf16[4,3,12,512]{3,2,1,0:T(8,128)(2,1)S(1)} %get-tuple-element.38), channel_id=1, source_target_pairs={{480,0},{0,32},{32,64},{64,96},{96,128},{128,160},{160,192},{192,2... | collective-permute-start | bytes 442376 | tf_op jit(solution)/shard_map/ppermute | solution.py:13
  108.5 150.0 %collective-permute-start.3 = (bf16[4,3,12,512]{3,0,2,1:T(4,128)(2,1)S(1)}, bf16[4,3,12,512]{3,0,2,1:T(4,128)(2,1)S(1)}, u32[]{:S(2)}, u32[]{:S(2)}) collective-permute-start(bf16[4,3,12,512]{3,0,2,1:T(4,128)(2,1)S(1)} %get-tuple-element.44), channel_id=1, source_target_pairs={{480,0},{0,32},{32,64},{64,96},{96,128},{128,160},{160,192},{192,2... | collective-permute-start | bytes 442376 | tf_op jit(solution)/shard_map/ppermute | solution.py:13
  159.5 412.6 %reduce-scatter.13.cloned.1.call-start = ((), (), s32[]{:S(2)}) async-start(), calls=%async_computation.6 | async-start | bytes 405504
Sparse Core Ops, SparseCore 0:
  65.4 92.5 reduce-scatter.10
  163.5 89.0 reduce-scatter.8
  255.6 155.7 reduce-scatter.14
  414.0 158.0 reduce-scatter.12
where the time goes:
time: 581 us; the launch traced here: 580 us
  waiting for transfers between devices  360 us (62%)
  blocking collectives  95.9 us (17%)
  local copies, waits for them, and re-layouts  36.1 us (6%)
  starting transfers between devices  35.5 us (6%)
  other arithmetic  19.6 us (3%)
  matrix products  18.9 us (3%)
  between operations  14.5 us (2%)
    unnamed x6, waiting for transfers between devices  311 us
    psum x1, blocking collectives, shards(): grad_bias = lax.psum(d_bias, ('lat', 'lon'))  95.9 us
    reduce_scatter x1, waiting for transfers between devices, shards(): lax.psum_scatter(d_wout.astype(jnp.bfloat16), 'lat', scatter_dimension=0,...  45.6 us
    ppermute x8, starting transfers between devices, passed_along(): return lax.ppermute(block, axis, route)  35.2 us
    unnamed x62, local copies, waits for them, and re-layouts  11.7 us
  transfers between devices with their start and end apart: 12, of which 4 were waited for; matrix products, arithmetic and copies ran while one was open for 8% of the time, Pallas kernels for 0%

commit v1 on v0

v1 whole, which is shorter than its diff:
```python
import jax
import jax.numpy as jnp
from jax import lax
from jax.experimental import pallas as pl
from jax.experimental.pallas import tpu as pltpu
from jax.sharding import PartitionSpec as P

MESH = pl.DeviceIdType.MESH
BF = jnp.bfloat16
F32 = jnp.float32
D = 512
HEADS = 8
HD = 64
WIN = 144
PART = 36
QROWS = 80
NX, NY, NZ = 4, 8, 8


def nn(a, b):
    return lax.dot_general(a, b, (((1,), (0,)), ((), ())), preferred_element_type=F32)


def nt(a, b):
    return lax.dot_general(a, b, (((1,), (1,)), ((), ())), preferred_element_type=F32)


def tn(a, b):
    return lax.dot_general(a, b, (((0,), (0,)), ((), ())), preferred_element_type=F32)


def iota(shape, axis):
    return lax.broadcasted_iota(jnp.int32, shape, axis)


def one_hot(cond):
    return jnp.where(cond, 1.0, 0.0).astype(BF)


def token_place(t):
    quad = (t >= 36).astype(jnp.int32) + (t >= 72).astype(jnp.int32) + (t >= 108).astype(jnp.int32)
    rem = t - 36 * quad
    lev = (rem >= 18).astype(jnp.int32)
    pos = rem - 18 * lev
    row = (pos >= 6).astype(jnp.int32) + (pos >= 12).astype(jnp.int32)
    return quad, lev, row, pos - 6 * row


def quad_row(s):
    w = (s >= WIN).astype(jnp.int32)
    t = s - WIN * w
    quad = (t >= 36).astype(jnp.int32) + (t >= 72).astype(jnp.int32) + (t >= 108).astype(jnp.int32)
    return quad * QROWS + w * PART + (t - 36 * quad)


def kernel(
    xq, cq, wqkv_h, wout_h, land, bias,
    out_att, out_tok, g_qkv, g_out, g_bias,
    hx, hc, wqkv, wout, wt, perm, sel, selt, normal, inv,
    normw, cotw, nmt, qkvt, dmt, mixt, mixp, dqkvt, r_q, r_o,
    oa, ot, core_s, core_r,
    a1, ra1, a2, ra2, a3, ra3, b1, rb1, b2, rb2, b3, rb3, c1, rc1, c2, rc2, c3, rc3,
    dbias, bc, bx, by, bz,
    lsem, hs, hr, os, orr, cs, cr, xs, xr, ys, yr, zs, zr,
):
    lat = lax.axis_index("lat")
    lon = lax.axis_index("lon")
    core = lat & 1
    px = (lat >> 1) & 3
    pzh = lat >> 3
    py = lon >> 2
    pzl = lon & 3
    pz = pzh * 4 + pzl

    def dev(x, y, z, c):
        return ((z >> 2) * 8 + x * 2 + c, y * 4 + (z & 3))

    def at_core():
        return dev(px, py, pz, 1 - core)

    def at_x(d):
        return dev((px + d) & 3, py, pz, core)

    def at_y(d):
        return dev(px, (py + d) & 7, pz, core)

    def at_z(d):
        return dev(px, py, (pz + d) & 7, core)

    back = [None, ((lat + 15) & 15, lon), (lat, (lon + 31) & 31), ((lat + 15) & 15, (lon + 31) & 31)]
    ahead = [None, ((lat + 1) & 15, lon), (lat, (lon + 1) & 31), ((lat + 1) & 15, (lon + 1) & 31)]

    w_copy = pltpu.make_async_copy(wqkv_h, wqkv, lsem.at[0])
    w_copy.start()
    o_copy = pltpu.make_async_copy(wout_h, wout, lsem.at[1])
    o_copy.start()

    barrier = pltpu.get_barrier_semaphore()
    partners = back[1:] + ahead[1:] + [at_core()]
    partners += [at_x(d) for d in range(1, NX)]
    partners += [at_y(d) for d in range(1, NY)] + [at_z(d) for d in range(1, NZ)]
    for where in partners:
        pl.semaphore_signal(barrier, inc=1, device_id=where, device_id_type=MESH)
    pl.semaphore_wait(barrier, len(partners))

    def send(src, dst, ssem, rsem, where):
        copy = pltpu.make_async_remote_copy(
            src_ref=src, dst_ref=dst, send_sem=ssem, recv_sem=rsem,
            device_id=where, device_id_type=MESH,
        )
        copy.start()
        return copy

    halo_x = [send(xq.at[q], hx.at[q - 1], hs.at[q - 1], hr.at[q - 1], back[q]) for q in (3, 1, 2)]
    halo_c = [send(cq.at[q], hc.at[q - 1], hs.at[q + 2], hr.at[q + 2], back[q]) for q in (3, 1, 2)]

    s_col = iota((2 * WIN, 1), 0)
    sel[...] = one_hot(iota((2 * WIN, 4 * QROWS), 1) == quad_row(s_col))
    for w in range(2):
        s_row = iota((1, WIN), 1) + w * WIN
        selt[w] = one_hot(iota((4 * QROWS, WIN), 0) == quad_row(s_row))
    r = iota((D, 1), 0)
    half = r >> 8
    a = r & 255
    is_a = a < 128
    is_b = a < 192
    b = a & 63
    f_x = jnp.where(is_a, a >> 5, jnp.where(is_b, b >> 4, (b >> 3) & 3))
    f_zh = jnp.where(is_a, (a >> 4) & 1, jnp.where(is_b, (b >> 3) & 1, b >> 5))
    f_i = jnp.where(is_a, a & 15, jnp.where(is_b, 16 + (b & 7), 24 + (b & 7)))
    f_c = jnp.where(half == 0, 1 - core, core)
    perm[...] = one_hot(iota((D, D), 1) == f_zh * 256 + f_x * 64 + f_c * 32 + f_i)
    r_q[...] = jnp.zeros_like(r_q)
    r_o[...] = jnp.zeros_like(r_o)

    quad, _, row, col = token_place(iota((WIN, 1), 0))
    l_row = lat * 6 + 3 + (quad & 1) * 3 + row
    l_row = jnp.where(l_row >= 96, l_row - 96, l_row)
    l_col = lon * 12 + 6 + (quad >> 1) * 6 + col
    l_col = jnp.where(l_col >= 384, l_col - 384, l_col)
    picked = nn(one_hot(iota((WIN, 96), 1) == l_row), land[...].astype(F32).astype(BF))
    land_key = jnp.sum(jnp.where(iota((WIN, 384), 1) == l_col, picked, 0.0), axis=1, keepdims=True)

    def region(t, w):
        quad, lev, _, _ = token_place(t)
        seam = jnp.where(lat == 15, 2, 0)
        return seam * (quad & 1) + (lev if w == 1 else 0)

    masks = [
        jnp.where(region(iota((WIN, 1), 0), w) == region(iota((1, WIN), 1), w), 0.0, -1e30)
        for w in range(2)
    ]

    w_copy.wait()
    o_copy.wait()
    eye = one_hot(iota((256, 256), 0) == iota((256, 256), 1))
    for k in range(6):
        wt[256 * k : 256 * k + 256] = nt(eye, wqkv[:, 256 * k : 256 * k + 256]).astype(BF)

    def layer_norm(x, q):
        x = x.astype(F32)
        centred = x - jnp.mean(x, axis=1, keepdims=True)
        scale = lax.rsqrt(jnp.mean(centred * centred, axis=1, keepdims=True) + 1e-05)
        normal[q] = centred * scale
        inv[q] = jnp.broadcast_to(scale, (QROWS, 128))

    layer_norm(xq[0], 0)
    for copy, q in zip(halo_x, (3, 1, 2)):
        copy.wait()
        layer_norm(hx[q - 1], q)
    normed = normal[...].reshape(4 * QROWS, D).astype(BF)
    normw[...] = nn(sel[...], normed).astype(BF)
    for w in range(2):
        nw = normw[WIN * w : WIN * w + WIN]
        qkvt[w] = nt(wt[...], nw).astype(BF)
        nmt[w] = nt(perm[...], nw).astype(BF)
    for copy in halo_c:
        copy.wait()
    cot = jnp.concatenate([cq[0], hc[0], hc[1], hc[2]], axis=0)
    cotw[...] = nn(sel[...], cot).astype(BF)
    for w in range(2):
        cw = cotw[WIN * w : WIN * w + WIN]
        dmt[w] = nt(wout[...], cw).astype(BF)
        for k in range(2):
            ct = nt(eye, cw[:, 256 * k : 256 * k + 256]).astype(BF)
            for g in range(16):
                at = 64 * (16 * k + g) + 48
                r_o[w, at : at + 16] = ct[16 * g : 16 * g + 16]

    def one_head(h, carry):
        base = pl.multiple_of(h * HD, HD)
        bias_h = bias[h]
        d_bias = jnp.zeros((1, WIN), F32)
        for w in range(2):
            qt = qkvt[w, pl.ds(base, HD)]
            kt = qkvt[w, pl.ds(D + base, HD)]
            vt = qkvt[w, pl.ds(2 * D + base, HD)]
            dm = dmt[w, pl.ds(base, HD)]
            score = tn(kt, qt) * (HD ** -0.5) + (bias_h * land_key + masks[w])
            expo = jnp.exp(score - jnp.max(score, axis=0, keepdims=True))
            prob = expo * (1.0 / jnp.sum(expo, axis=0, keepdims=True))
            prob_b = prob.astype(BF)
            mixt[w, pl.ds(base, HD)] = nn(vt, prob_b).astype(BF)
            d_prob = tn(vt, dm).astype(BF).astype(F32)
            d_v = nt(dm, prob_b).astype(BF)
            d_score = prob * (d_prob - jnp.sum(prob * d_prob, axis=0, keepdims=True))
            d_bias = d_bias + jnp.sum(d_score * land_key, axis=0, keepdims=True)
            ds_b = d_score.astype(BF)
            d_q = (nn(kt, ds_b) * (HD ** -0.5)).astype(BF)
            d_k = (nt(qt, ds_b) * (HD ** -0.5)).astype(BF)
            for part, grad in enumerate((d_q, d_k, d_v)):
                dqkvt[w, pl.ds(part * D + base, HD)] = grad
                for g in range(4):
                    piece = h * 4 + (part * 32 + g)
                    at = pl.multiple_of((piece // 3) * 64 + (piece % 3) * 16, 16)
                    r_q[w, pl.ds(at, 16)] = grad[16 * g : 16 * g + 16]
        dbias[pl.ds(h, 1)] = d_bias
        return carry

    lax.fori_loop(0, HEADS, one_head, 0)

    bc[0] = jnp.broadcast_to(jnp.sum(dbias[...], axis=1, keepdims=True), (HEADS, 128))
    bias_c = send(bc.at[0], bc.at[1], cs.at[0], cr.at[0], at_core())

    for w in range(2):
        mixp[w] = nn(perm[...], mixt[w]).astype(BF)

    def grad_block(first, y):
        cols = pl.ds(pl.multiple_of(y * 256, 256), 256)
        total = None
        for w in range(2):
            for left, right in ((nmt, r_q), (mixp, r_o)):
                term = nt(left[w, first : first + 256], right[w, cols])
                total = term if total is None else total + term
        return total

    def partner_block(y, carry):
        core_s[y] = grad_block(0, y).astype(BF)
        return carry

    lax.fori_loop(0, NY, partner_block, 0)
    core_copy = send(core_s, core_r, cs.at[1], cr.at[1], at_core())

    core_copy.wait()
    lane_low = iota((64, 128), 1) < 64
    kept = []
    for y in range(NY):
        total = grad_block(256, y) + core_r[y].astype(F32)
        for x in range(NX):
            a1[x, y] = total[32 * x : 32 * x + 32].astype(BF)
        b1[y] = total[128:192].astype(BF)
        kept.append(total[192:256])
        if y % 2 == 1:
            m = y // 2
            for t in range(2):
                lo = kept[0][:, 128 * t : 128 * t + 128]
                hi = kept[1][:, 128 * t : 128 * t + 128]
                even = jnp.where(lane_low, lo, pltpu.roll(hi, 64, 1)).astype(BF)
                odd = jnp.where(lane_low, pltpu.roll(lo, 64, 1), hi).astype(BF)
                for zh in range(2):
                    c1[zh * 4 + 2 * t, :, 128 * m : 128 * m + 128] = even[32 * zh : 32 * zh + 32]
                    c1[zh * 4 + 2 * t + 1, :, 128 * m : 128 * m + 128] = odd[32 * zh : 32 * zh + 32]
            kept = []

    def swap_x(src, dst, stage):
        return [send(src(d), dst.at[d - 1], xs.at[stage, d - 1], xr.at[stage, d - 1], at_x(d)) for d in (2, 1, 3)]

    def swap_y(src, dst, stage):
        return [send(src(d), dst.at[d - 1], ys.at[stage, d - 1], yr.at[stage, d - 1], at_y(d)) for d in (4, 3, 5, 2, 6, 1, 7)]

    def swap_z(src, dst, stage):
        return [send(src(d), dst.at[d - 1], zs.at[stage, d - 1], zr.at[stage, d - 1], at_z(d)) for d in (4, 3, 5, 2, 6, 1, 7)]

    def wait(copies):
        for copy in copies:
            copy.wait()

    def summed(own_part, parts, count):
        total = own_part.astype(F32)
        for d in range(count):
            total = total + parts[d].astype(F32)
        return total

    go_a = swap_x(lambda d: a1.at[(px + d) & 3], ra1, 0)
    go_b = swap_y(lambda d: b1.at[(py + d) & 7], rb1, 0)
    go_c = swap_z(lambda d: c1.at[(pz + d) & 7], rc1, 0)
    bias_c.wait()
    bx[0] = bc[0] + bc[1]
    go_bias = [send(bx.at[0], bx.at[d], xs.at[3, d - 1], xr.at[3, d - 1], at_x(d)) for d in (2, 1, 3)]

    out_sends = []
    for q in (3, 1, 2, 0):
        rows = slice(QROWS * q, QROWS * q + QROWS)
        mixed = (nt(selt[0, rows], mixt[0]) + nt(selt[1, rows], mixt[1])).astype(BF)
        att = nn(mixed, wout[...]).astype(BF)
        if q == 0:
            out_att[0] = att
        else:
            oa[q - 1] = att
            out_sends.append(send(oa.at[q - 1], out_att.at[q], os.at[q - 1], orr.at[q - 1], ahead[q]))
        d_qkv = (nt(selt[0, rows], dqkvt[0]) + nt(selt[1, rows], dqkvt[1])).astype(BF)
        d_normed = nn(d_qkv, wt[...])
        norm = normal[q]
        mean_grad = jnp.mean(d_normed, axis=1, keepdims=True)
        mean_cross = jnp.mean(d_normed * norm, axis=1, keepdims=True)
        d_tok = (inv[q][:, 0:1] * (d_normed - mean_grad - norm * mean_cross)).astype(BF)
        if q == 0:
            out_tok[0] = d_tok
        else:
            ot[q - 1] = d_tok
            out_sends.append(send(ot.at[q - 1], out_tok.at[q], os.at[q + 2], orr.at[q + 2], ahead[q]))

    wait(go_a)
    for y in range(NY):
        total = a1[px, y].astype(F32)
        for d in range(3):
            total = total + ra1[d, y].astype(F32)
        a2[y] = total.astype(BF)
    go_a = swap_y(lambda d: a2.at[(py + d) & 7], ra2, 1)
    wait(go_b)
    total = summed(b1[py], rb1, 7)
    for zh in range(2):
        for t in range(2):
            for x in range(NX):
                at = 16 * x + 8 * zh
                b2[zh * 2 + t, 8 * x : 8 * x + 8] = total[at : at + 8, 128 * t : 128 * t + 128]
    go_b = swap_z(lambda d: b2.at[((pz + d) & 7) >> 1], rb2, 1)
    wait(go_c)
    total = summed(c1[pz], rc1, 7)
    for x in range(NX):
        c2[x] = total[8 * x : 8 * x + 8]
    go_c = swap_x(lambda d: c2.at[(px + d) & 3], rc2, 1)
    wait(go_bias)

    def ordered(slots, me, n):
        total = slots[me & (n - 1)]
        for k in range(1, n):
            total = total + slots[(me - k) & (n - 1)]
        return total

    by[0] = ordered(bx, px, NX)
    go_bias = [send(by.at[0], by.at[d], ys.at[3, d - 1], yr.at[3, d - 1], at_y(d)) for d in (4, 3, 5, 2, 6, 1, 7)]

    wait(go_a)
    total = summed(a2[py], ra2, 7)
    for zh in range(2):
        for t in range(2):
            a3[zh * 2 + t] = total[16 * zh : 16 * zh + 16, 128 * t : 128 * t + 128]
    go_a = swap_z(lambda d: a3.at[((pz + d) & 7) >> 1], ra3, 2)
    wait(go_b)
    total = summed(b2[pz >> 1], rb2, 7)
    for x in range(NX):
        b3[x] = total[8 * x : 8 * x + 8]
    go_b = swap_x(lambda d: b3.at[(px + d) & 3], rb3, 2)
    wait(go_c)
    total = summed(c2[px], rc2, 3)
    for m in range(4):
        c3[m] = total[:, 128 * m : 128 * m + 128]
    go_c = swap_y(lambda d: c3.at[((py + d) & 7) >> 1], rc3, 2)
    wait(go_bias)
    bz[0] = ordered(by, py, NY)
    go_bias = [send(bz.at[0], bz.at[d], zs.at[3, d - 1], zr.at[3, d - 1], at_z(d)) for d in (4, 3, 5, 2, 6, 1, 7)]

    def mine(total, odd):
        return jnp.where(odd == 1, pltpu.roll(total, 64, 1), total)

    def put(first, total):
        count = total.shape[0]
        g_qkv[first : first + count] = total[:, 0:48]
        g_out[first : first + count] = total[:, 48:64]

    wait(go_a)
    put(0, mine(summed(a3[pz >> 1], ra3, 7), pzl & 1))
    wait(go_b)
    put(16, mine(summed(b3[px], rb3, 3), pzl & 1))
    wait(go_c)
    put(24, mine(summed(c3[py >> 1], rc3, 7), py & 1))
    wait(go_bias)
    g_bias[...] = ordered(bz, pz, NZ)
    wait(out_sends)


def to_quads(grid):
    moved = jnp.concatenate([grid[1:], grid[:1]], axis=0)
    quads = []
    for lon_part in (1, 0):
        for lat_part in (1, 0):
            block = moved[:, 3 * lat_part : 3 * lat_part + 3, 6 * lon_part : 6 * lon_part + 6]
            quads.append(jnp.pad(block.reshape(72, D), ((0, QROWS - 72), (0, 0))))
    return jnp.stack(quads)


def from_quads(quads):
    q = quads[:, :72].reshape(4, 4, 3, 6, D)
    high = jnp.concatenate([q[3], q[1]], axis=2)
    low = jnp.concatenate([q[2], q[0]], axis=2)
    grid = jnp.concatenate([high, low], axis=1)
    return jnp.concatenate([grid[3:], grid[:3]], axis=0)


def shards(tokens, cotangent, w_qkv, w_out, land_mask, land_bias):
    vmem = pl.BlockSpec(memory_space=pltpu.VMEM)
    anywhere = pl.BlockSpec(memory_space=pl.ANY)
    V = pltpu.VMEM
    dma = pltpu.SemaphoreType.DMA
    att, tok, g_qkv, g_out, g_bias = pl.pallas_call(
        kernel,
        out_shape=[
            jax.ShapeDtypeStruct((4, QROWS, D), BF),
            jax.ShapeDtypeStruct((4, QROWS, D), BF),
            jax.ShapeDtypeStruct((32, 48), F32),
            jax.ShapeDtypeStruct((32, 16), F32),
            jax.ShapeDtypeStruct((HEADS, 128), F32),
        ],
        in_specs=[vmem, vmem, anywhere, anywhere, vmem, pl.BlockSpec(memory_space=pltpu.SMEM)],
        out_specs=[vmem] * 5,
        scratch_shapes=[
            V((3, QROWS, D), BF), V((3, QROWS, D), BF),
            V((D, 3 * D), BF), V((D, D), BF), V((3 * D, D), BF),
            V((D, D), BF), V((2 * WIN, 4 * QROWS), BF), V((2, 4 * QROWS, WIN), BF),
            V((4, QROWS, D), F32), V((4, QROWS, 128), F32),
            V((2 * WIN, D), BF), V((2 * WIN, D), BF),
            V((2, D, WIN), BF), V((2, 3 * D, WIN), BF), V((2, D, WIN), BF),
            V((2, D, WIN), BF), V((2, D, WIN), BF), V((2, 3 * D, WIN), BF),
            V((2, 4 * D, WIN), BF), V((2, 4 * D, WIN), BF),
            V((3, QROWS, D), BF), V((3, QROWS, D), BF),
            V((NY, 256, 256), BF), V((NY, 256, 256), BF),
            V((NX, NY, 32, 256), BF), V((3, NY, 32, 256), BF),
            V((NY, 32, 256), BF), V((7, 32, 256), BF),
            V((4, 16, 128), F32), V((7, 16, 128), F32),
            V((NY, 64, 256), BF), V((7, 64, 256), BF),
            V((4, 32, 128), F32), V((7, 32, 128), F32),
            V((NX, 8, 128), F32), V((3, 8, 128), F32),
            V((NZ, 32, 512), BF), V((7, 32, 512), BF),
            V((NX, 8, 512), F32), V((3, 8, 512), F32),
            V((4, 8, 128), F32), V((7, 8, 128), F32),
            V((HEADS, WIN), F32), V((2, HEADS, 128), F32),
            V((NX, HEADS, 128), F32), V((NY, HEADS, 128), F32), V((NZ, HEADS, 128), F32),
            dma((2,)), dma((6,)), dma((6,)), dma((6,)), dma((6,)),
            dma((2,)), dma((2,)),
            dma((4, 3)), dma((4, 3)), dma((4, 7)), dma((4, 7)), dma((4, 7)), dma((4, 7)),
        ],
        compiler_params=pltpu.CompilerParams(
            collective_id=0, has_side_effects=True, vmem_limit_bytes=48 << 20
        ),
        name="swin_block",
    )(to_quads(tokens), to_quads(cotangent), w_qkv, w_out, land_mask, land_bias)
    return from_quads(att), from_quads(tok), g_qkv, g_out, g_bias[:, 0]


def solution(mesh):
    in_specs = (P(None, "lat", "lon", None), P(None, "lat", "lon", None), P(), P(), P(), P())
    out_specs = (
        P(None, "lat", "lon", None),
        P(None, "lat", "lon", None),
        P("lat", "lon"),
        P("lat", "lon"),
        P(),
    )
    return jax.shard_map(shards, mesh=mesh, in_specs=in_specs, out_specs=out_specs, check_vma=False)
```

time: 581 us -> 85.5 us (0.15)
  waiting for transfers between devices: 360 us -> 0 us
  blocking collectives: 95.9 us -> 0 us
  Pallas kernels: 0 us -> 73.3 us
  starting transfers between devices: 35.5 us -> 0 us
  local copies, waits for them, and re-layouts: 36.1 us -> 9.07 us
  matrix products: 18.9 us -> 0 us
  other arithmetic: 19.6 us -> 0.98 us
  between operations: 14.5 us -> 0.96 us
    unnamed x6 -> x0, waiting for transfers between devices: 311 us -> none
    psum x1 -> x0, blocking collectives: 95.9 us -> none  [shards(): grad_bias = lax.psum(d_bias, ('lat', 'lon'))]
    pallas_call x0 -> x1, Pallas kernels: none -> 73.3 us  [shards(): pl.pallas_call(kernel, out_shape=[jax.ShapeDtypeStruct((4, QROWS, D), BF)...]
    reduce_scatter x2 -> x0, waiting for transfers between devices: 45.6 us -> none  [the longest x1 45.6 us: shards(): lax.psum_scatter(d_wout.astype(jnp.bfloat16), 'lat', scatter_dimension=0,...]
    ppermute x8 -> x0, starting transfers between devices: 35.2 us -> none  [passed_along(): return lax.ppermute(block, axis, route)]
    dot_general x12 -> x0, matrix products: 18.9 us -> none  [the longest x3 5.41 us: window_attention(): jnp.einsum('bqhd,bkhd->bhqk', queries, key_vecs) * head_size ** (-0.5)]
    unnamed x62 -> x14, local copies, waits for them, and re-layouts: 11.7 us -> 4.27 us
    reduce_sum x6 -> x0, other arithmetic: 6.64 us -> none  [the longest x1 2.42 us: window_attention(): scores + land_bias[None, :, None, None] * land.astype(jnp.float32)[:, Non...]
  transfers between devices with their start and end apart: 12 -> 0, of which waited for: 4 -> 0; matrix products, arithmetic and copies ran while one was open for 8% -> 0% of each run, Pallas kernels for 0% -> 0%
where the time goes in v1:
time: 85.5 us; the launch traced here: 84.3 us
  Pallas kernels  73.3 us (86%)
  local copies, waits for them, and re-layouts  9.07 us (11%)
  other arithmetic  0.98 us (1%)
  between operations  0.96 us (1%)
    pallas_call x1, Pallas kernels, shards(): pl.pallas_call(kernel, out_shape=[jax.ShapeDtypeStruct((4, QROWS, D), BF)...  73.3 us
    unnamed x14, local copies, waits for them, and re-layouts  4.27 us
    slice x4, local copies, waits for them, and re-layouts, to_quads(): moved = jnp.concatenate([grid[1:], grid[:1]], axis=0)  3.42 us

profile of v1, /device:TPU:6, one launch (start us, length us, event | category | flops | bytes accessed | tf_op | source)
XLA Modules:
  0.0 84.3 jit_solution(3759684326463821163)
XLA Ops:
  0.6 1.1 %slice.94 = bf16[1,6,12,512]{3,0,2,1:T(2,128)(2,1)S(1)} slice(bf16[4,6,12,512]{3,0,2,1:T(4,128)(2,1)} %param.6), slice={[0:1], [0:6], [0:12], [0:512]} | slice | bytes 147456 | tf_op jit(solution)/shard_map/slice | solution.py:384
  1.7 1.1 %slice.100 = bf16[1,6,12,512]{3,0,2,1:T(2,128)(2,1)S(1)} slice(bf16[4,6,12,512]{3,0,2,1:T(4,128)(2,1)} %param.7), slice={[0:1], [0:6], [0:12], [0:512]} | slice | bytes 147456 | tf_op jit(solution)/shard_map/slice | solution.py:384
  2.8 1.1 %slice.93 = bf16[3,6,12,512]{3,0,2,1:T(4,128)(2,1)S(1)} slice(bf16[4,6,12,512]{3,0,2,1:T(4,128)(2,1)} %param.6), slice={[1:4], [0:6], [0:12], [0:512]} | slice | bytes 442368 | tf_op jit(solution)/shard_map/slice | solution.py:384
  3.9 0.0 copy-start.4
  3.9 0.3 fusion.10
  4.6 0.3 copy-done.4
  4.9 0.2 slice.99
  5.0 0.0 copy-start
  5.0 0.0 copy-start.1
  5.1 0.0 copy-start.2
  5.1 0.0 copy-start.3
  5.1 0.3 fusion.7
  5.8 0.7 copy-done
  6.4 0.1 copy-done.1
  6.5 0.0 copy-done.2
  6.6 0.0 copy-done.3
  6.6 73.3 %swin_block.1 = (bf16[4,80,512]{2,1,0:T(8,128)(2,1)S(1)}, bf16[4,80,512]{2,1,0:T(8,128)(2,1)S(1)}, f32[32,48]{1,0:T(8,128)S(1)}, f32[32,16]{1,0:T(8,128)S(1)}, f32[8,128]{1,0:T(8,128)S(1)}) custom-call(bf16[4,80,512]{2,1,0:T(8,128)(2,1)S(1)} %pad_maximum_fusion.8.xq, bf16[4,80,512]{2,1,0:T(8,128)(2,1)S(1)} %pad_maximum_fusion.9.cq, ...), custom_call_target="tpu_custom_call" | custom-call | tf_op jit(solution)/shard_map/swin_block/pallas_call | solution.py:406
  79.9 0.6 slice_reduce_fusion
  80.5 0.7 copy.38
  81.3 0.1 fusion.4
  81.5 0.9 %copy.36 = bf16[4,6,12,512]{3,0,2,1:T(4,128)(2,1)} copy(bf16[4,6,12,512]{3,2,1,0:T(8,128)(2,1)S(1)} %fusion.4) | data formatting | bytes 589824
  82.6 0.1 fusion.1
  82.7 0.9 %copy.37 = bf16[4,6,12,512]{3,0,2,1:T(4,128)(2,1)} copy(bf16[4,6,12,512]{3,2,1,0:T(8,128)(2,1)S(1)} %fusion.1) | data formatting | bytes 589824
  83.7 0.6 copy.40
  (32 shorter events, 0.8 us)
Async XLA Ops:
  3.9 1.0 %copy-start.4 = (bf16[4,6,12,512]{3,0,2,1:T(4,128)(2,1)S(1)}, bf16[4,6,12,512]{3,0,2,1:T(4,128)(2,1)}, u32[]{:S(2)}) copy-start(bf16[4,6,12,512]{3,0,2,1:T(4,128)(2,1)} %param.7) | copy-start | bytes 884740
  5.0 1.4 %copy-start = (bf16[512,1536]{1,0:T(8,128)(2,1)S(1)}, bf16[512,1536]{1,0:T(8,128)(2,1)}, u32[]{:S(2)}) copy-start(bf16[512,1536]{1,0:T(8,128)(2,1)} %wqkv_h.1) | copy-start | bytes 4718596
  5.0 1.5 %copy-start.1 = (bf16[512,512]{1,0:T(8,128)(2,1)S(1)}, bf16[512,512]{1,0:T(8,128)(2,1)}, u32[]{:S(2)}) copy-start(bf16[512,512]{1,0:T(8,128)(2,1)} %wout_h.1) | copy-start | bytes 1572868
  5.1 1.5 %copy-start.2 = (s32[96,384]{1,0:T(8,128)S(1)}, s32[96,384]{1,0:T(8,128)}, u32[]{:S(2)}) copy-start(s32[96,384]{1,0:T(8,128)} %land.1) | copy-start | bytes 442372
  5.1 1.5 %copy-start.3 = (f32[8]{0:T(128)S(1)}, f32[8]{0:T(128)}, u32[]{:S(2)}) copy-start(f32[8]{0:T(128)} %bias.1) | copy-start | bytes 100

commit v2 on v1

--- a/solution.py
+++ b/solution.py
@@ -13,6 +13,8 @@
 HD = 64
 WIN = 144
 PART = 36
+CELLS = 72
+PADDED = CELLS * 16
 QROWS = 80
 NX, NY, NZ = 4, 8, 8
 
@@ -53,10 +55,23 @@
     return quad * QROWS + w * PART + (t - 36 * quad)
 
 
+def grid_row(s):
+    quad = (s >= QROWS).astype(jnp.int32) + (s >= 2 * QROWS).astype(jnp.int32) + (s >= 3 * QROWS).astype(jnp.int32)
+    rem = s - QROWS * quad
+    step = (rem >= 18).astype(jnp.int32) + (rem >= 36).astype(jnp.int32) + (rem >= 54).astype(jnp.int32)
+    pos = rem - 18 * step
+    row = (pos >= 6).astype(jnp.int32) + (pos >= 12).astype(jnp.int32)
+    col = pos - 6 * row
+    lev = (step + 1) & 3
+    at = ((3 * (1 - (quad & 1)) + row) * 12 + 6 * (1 - (quad >> 1)) + col) * 16 + lev
+    return jnp.where(rem < 72, at, -1)
+
+
 def kernel(
-    xq, cq, wqkv_h, wout_h, land, bias,
+    tok_h, cot_h, wqkv_h, wout_h, land, bias,
     out_att, out_tok, g_qkv, g_out, g_bias,
-    hx, hc, wqkv, wout, wt, perm, sel, selt, normal, inv,
+    tok_v, cot_v, raw, xq, cq, hx, hc, att_q, tok_q, spread,
+    wqkv, wout, wt, perm, sel, selt, normal, inv,
     normw, cotw, nmt, qkvt, dmt, mixt, mixp, dqkvt, r_q, r_o,
     oa, ot, core_s, core_r,
     a1, ra1, a2, ra2, a3, ra3, b1, rb1, b2, rb2, b3, rb3, c1, rc1, c2, rc2, c3, rc3,
@@ -90,17 +105,29 @@
     back = [None, ((lat + 15) & 15, lon), (lat, (lon + 31) & 31), ((lat + 15) & 15, (lon + 31) & 31)]
     ahead = [None, ((lat + 1) & 15, lon), (lat, (lon + 1) & 31), ((lat + 1) & 15, (lon + 1) & 31)]
 
-    w_copy = pltpu.make_async_copy(wqkv_h, wqkv, lsem.at[0])
-    w_copy.start()
-    o_copy = pltpu.make_async_copy(wout_h, wout, lsem.at[1])
-    o_copy.start()
-
     barrier = pltpu.get_barrier_semaphore()
     partners = back[1:] + ahead[1:] + [at_core()]
     partners += [at_x(d) for d in range(1, NX)]
     partners += [at_y(d) for d in range(1, NY)] + [at_z(d) for d in range(1, NZ)]
     for where in partners:
         pl.semaphore_signal(barrier, inc=1, device_id=where, device_id_type=MESH)
+
+    t_copy = pltpu.make_async_copy(tok_h, tok_v, lsem.at[2])
+    t_copy.start()
+    c_copy = pltpu.make_async_copy(cot_h, cot_v, lsem.at[3])
+    c_copy.start()
+    w_copy = pltpu.make_async_copy(wqkv_h, wqkv, lsem.at[0])
+    w_copy.start()
+    o_copy = pltpu.make_async_copy(wout_h, wout, lsem.at[1])
+    o_copy.start()
+    raw[...] = jnp.zeros_like(raw)
+    spread[...] = one_hot(iota((PADDED, 4 * QROWS), 0) == grid_row(iota((1, 4 * QROWS), 1)))
+    cut = one_hot(grid_row(iota((4 * QROWS, 1), 0)) == iota((4 * QROWS, PADDED), 1))
+    for copy, held, quads in ((t_copy, tok_v, xq), (c_copy, cot_v, cq)):
+        copy.wait()
+        raw[:, 0:4, :] = held[...]
+        grid = raw[...].reshape(PADDED, D)
+        quads[...] = nn(cut, grid).astype(BF).reshape(4, QROWS, D)
     pl.semaphore_wait(barrier, len(partners))
 
     def send(src, dst, ssem, rsem, where):
@@ -187,8 +214,8 @@
                 at = 64 * (16 * k + g) + 48
                 r_o[w, at : at + 16] = ct[16 * g : 16 * g + 16]
 
-    def one_head(h, carry):
-        base = pl.multiple_of(h * HD, HD)
+    def one_head(h):
+        base = h * HD
         bias_h = bias[h]
         d_bias = jnp.zeros((1, WIN), F32)
         for w in range(2):
@@ -212,12 +239,12 @@
                 dqkvt[w, pl.ds(part * D + base, HD)] = grad
                 for g in range(4):
                     piece = h * 4 + (part * 32 + g)
-                    at = pl.multiple_of((piece // 3) * 64 + (piece % 3) * 16, 16)
+                    at = (piece // 3) * 64 + (piece % 3) * 16
                     r_q[w, pl.ds(at, 16)] = grad[16 * g : 16 * g + 16]
-        dbias[pl.ds(h, 1)] = d_bias
-        return carry
-
-    lax.fori_loop(0, HEADS, one_head, 0)
+        dbias[h : h + 1] = d_bias
+
+    for h in range(HEADS):
+        one_head(h)
 
     bc[0] = jnp.broadcast_to(jnp.sum(dbias[...], axis=1, keepdims=True), (HEADS, 128))
     bias_c = send(bc.at[0], bc.at[1], cs.at[0], cr.at[0], at_core())
@@ -226,7 +253,7 @@
         mixp[w] = nn(perm[...], mixt[w]).astype(BF)
 
     def grad_block(first, y):
-        cols = pl.ds(pl.multiple_of(y * 256, 256), 256)
+        cols = slice(y * 256, y * 256 + 256)
         total = None
         for w in range(2):
             for left, right in ((nmt, r_q), (mixp, r_o)):
@@ -234,17 +261,32 @@
                 total = term if total is None else total + term
         return total
 
-    def partner_block(y, carry):
+    core_copies = []
+    for y in range(NY):
         core_s[y] = grad_block(0, y).astype(BF)
-        return carry
-
-    lax.fori_loop(0, NY, partner_block, 0)
-    core_copy = send(core_s, core_r, cs.at[1], cr.at[1], at_core())
-
-    core_copy.wait()
+        if y % 2 == 1:
+            pair, k = slice(y - 1, y + 1), 1 + y // 2
+            core_copies.append(send(core_s.at[pair], core_r.at[pair], cs.at[k], cr.at[k], at_core()))
+
+    out_sends = []
+
+    def give(q, value, mine, away, far, k):
+        if q == 0:
+            mine[0] = value
+        else:
+            away[q - 1] = value
+            out_sends.append(send(away.at[q - 1], far.at[q], os.at[k], orr.at[k], ahead[q]))
+
+    for q in (3, 1, 2, 0):
+        rows = slice(QROWS * q, QROWS * q + QROWS)
+        mixed = (nt(selt[0, rows], mixt[0]) + nt(selt[1, rows], mixt[1])).astype(BF)
+        give(q, nn(mixed, wout[...]).astype(BF), att_q, oa, att_q, q - 1)
+
     lane_low = iota((64, 128), 1) < 64
     kept = []
     for y in range(NY):
+        if y % 2 == 0:
+            core_copies[y // 2].wait()
         total = grad_block(256, y) + core_r[y].astype(F32)
         for x in range(NX):
             a1[x, y] = total[32 * x : 32 * x + 32].astype(BF)
@@ -281,34 +323,22 @@
             total = total + parts[d].astype(F32)
         return total
 
+    go_c = swap_z(lambda d: c1.at[(pz + d) & 7], rc1, 0)
+    go_b = swap_y(lambda d: b1.at[(py + d) & 7], rb1, 0)
     go_a = swap_x(lambda d: a1.at[(px + d) & 3], ra1, 0)
-    go_b = swap_y(lambda d: b1.at[(py + d) & 7], rb1, 0)
-    go_c = swap_z(lambda d: c1.at[(pz + d) & 7], rc1, 0)
     bias_c.wait()
     bx[0] = bc[0] + bc[1]
     go_bias = [send(bx.at[0], bx.at[d], xs.at[3, d - 1], xr.at[3, d - 1], at_x(d)) for d in (2, 1, 3)]
 
-    out_sends = []
     for q in (3, 1, 2, 0):
         rows = slice(QROWS * q, QROWS * q + QROWS)
-        mixed = (nt(selt[0, rows], mixt[0]) + nt(selt[1, rows], mixt[1])).astype(BF)
-        att = nn(mixed, wout[...]).astype(BF)
-        if q == 0:
-            out_att[0] = att
-        else:
-            oa[q - 1] = att
-            out_sends.append(send(oa.at[q - 1], out_att.at[q], os.at[q - 1], orr.at[q - 1], ahead[q]))
         d_qkv = (nt(selt[0, rows], dqkvt[0]) + nt(selt[1, rows], dqkvt[1])).astype(BF)
         d_normed = nn(d_qkv, wt[...])
         norm = normal[q]
         mean_grad = jnp.mean(d_normed, axis=1, keepdims=True)
         mean_cross = jnp.mean(d_normed * norm, axis=1, keepdims=True)
         d_tok = (inv[q][:, 0:1] * (d_normed - mean_grad - norm * mean_cross)).astype(BF)
-        if q == 0:
-            out_tok[0] = d_tok
-        else:
-            ot[q - 1] = d_tok
-            out_sends.append(send(ot.at[q - 1], out_tok.at[q], os.at[q + 2], orr.at[q + 2], ahead[q]))
+        give(q, d_tok, tok_q, ot, tok_q, q + 2)
 
     wait(go_a)
     for y in range(NY):
@@ -364,38 +394,38 @@
     def mine(total, odd):
         return jnp.where(odd == 1, pltpu.roll(total, 64, 1), total)
 
-    def put(first, total):
-        count = total.shape[0]
-        g_qkv[first : first + count] = total[:, 0:48]
-        g_out[first : first + count] = total[:, 48:64]
+    wait(out_sends)
+    for quads, out in ((att_q, out_att), (tok_q, out_tok)):
+        grid = nn(spread[...], quads[...].reshape(4 * QROWS, D)).astype(BF)
+        out[...] = grid.reshape(CELLS, 16, D)[:, 0:4, :]
 
     wait(go_a)
-    put(0, mine(summed(a3[pz >> 1], ra3, 7), pzl & 1))
+    grad_a = mine(summed(a3[pz >> 1], ra3, 7), pzl & 1)
     wait(go_b)
-    put(16, mine(summed(b3[px], rb3, 3), pzl & 1))
+    grad_b = mine(summed(b3[px], rb3, 3), pzl & 1)
     wait(go_c)
-    put(24, mine(summed(c3[py >> 1], rc3, 7), py & 1))
+    grad_c = mine(summed(c3[py >> 1], rc3, 7), py & 1)
+    grads = jnp.concatenate([grad_a, grad_b, grad_c], axis=0)
+    g_qkv[...] = grads[:, 0:48]
+    g_out[...] = grads.T[48:64]
     wait(go_bias)
-    g_bias[...] = ordered(bz, pz, NZ)
-    wait(out_sends)
-
-
-def to_quads(grid):
-    moved = jnp.concatenate([grid[1:], grid[:1]], axis=0)
-    quads = []
-    for lon_part in (1, 0):
-        for lat_part in (1, 0):
-            block = moved[:, 3 * lat_part : 3 * lat_part + 3, 6 * lon_part : 6 * lon_part + 6]
-            quads.append(jnp.pad(block.reshape(72, D), ((0, QROWS - 72), (0, 0))))
-    return jnp.stack(quads)
-
-
-def from_quads(quads):
-    q = quads[:, :72].reshape(4, 4, 3, 6, D)
-    high = jnp.concatenate([q[3], q[1]], axis=2)
-    low = jnp.concatenate([q[2], q[0]], axis=2)
-    grid = jnp.concatenate([high, low], axis=1)
-    return jnp.concatenate([grid[3:], grid[:3]], axis=0)
+    total = ordered(bz, pz, NZ)
+    on_diagonal = iota((HEADS, 128), 0) == iota((HEADS, 128), 1)
+    g_bias[...] = jnp.sum(jnp.where(on_diagonal, total, 0.0), axis=0, keepdims=True)[:, 0:HEADS]
+
+
+def place(*refs):
+    count = len(refs) // 2
+    for k in range(count):
+        refs[count + k][...] = refs[k][...]
+
+
+def cells(grid):
+    return grid.transpose(1, 2, 0, 3).reshape(CELLS, 4, D)
+
+
+def levels(grid):
+    return grid.reshape(6, 12, 4, D).transpose(2, 0, 1, 3)
 
 
 def shards(tokens, cotangent, w_qkv, w_out, land_mask, land_bias):
@@ -406,16 +436,19 @@
     att, tok, g_qkv, g_out, g_bias = pl.pallas_call(
         kernel,
         out_shape=[
-            jax.ShapeDtypeStruct((4, QROWS, D), BF),
-            jax.ShapeDtypeStruct((4, QROWS, D), BF),
+            jax.ShapeDtypeStruct((CELLS, 4, D), BF),
+            jax.ShapeDtypeStruct((CELLS, 4, D), BF),
             jax.ShapeDtypeStruct((32, 48), F32),
-            jax.ShapeDtypeStruct((32, 16), F32),
-            jax.ShapeDtypeStruct((HEADS, 128), F32),
+            jax.ShapeDtypeStruct((16, 32), F32),
+            jax.ShapeDtypeStruct((1, HEADS), F32),
         ],
-        in_specs=[vmem, vmem, anywhere, anywhere, vmem, pl.BlockSpec(memory_space=pltpu.SMEM)],
+        in_specs=[anywhere, anywhere, anywhere, anywhere, vmem, pl.BlockSpec(memory_space=pltpu.SMEM)],
         out_specs=[vmem] * 5,
         scratch_shapes=[
+            V((CELLS, 4, D), BF), V((CELLS, 4, D), BF), V((CELLS, 16, D), BF),
+            V((4, QROWS, D), BF), V((4, QROWS, D), BF),
             V((3, QROWS, D), BF), V((3, QROWS, D), BF),
+            V((4, QROWS, D), BF), V((4, QROWS, D), BF), V((PADDED, 4 * QROWS), BF),
             V((D, 3 * D), BF), V((D, D), BF), V((3 * D, D), BF),
             V((D, D), BF), V((2 * WIN, 4 * QROWS), BF), V((2, 4 * QROWS, WIN), BF),
             V((4, QROWS, D), F32), V((4, QROWS, 128), F32),
@@ -436,16 +469,25 @@
             V((4, 8, 128), F32), V((7, 8, 128), F32),
             V((HEADS, WIN), F32), V((2, HEADS, 128), F32),
             V((NX, HEADS, 128), F32), V((NY, HEADS, 128), F32), V((NZ, HEADS, 128), F32),
-            dma((2,)), dma((6,)), dma((6,)), dma((6,)), dma((6,)),
-            dma((2,)), dma((2,)),
+            dma((4,)), dma((6,)), dma((6,)), dma((6,)), dma((6,)),
+            dma((5,)), dma((5,)),
             dma((4, 3)), dma((4, 3)), dma((4, 7)), dma((4, 7)), dma((4, 7)), dma((4, 7)),
         ],
         compiler_params=pltpu.CompilerParams(
-            collective_id=0, has_side_effects=True, vmem_limit_bytes=48 << 20
+            collective_id=0, has_side_effects=True, vmem_limit_bytes=60 << 20
         ),
         name="swin_block",
-    )(to_quads(tokens), to_quads(cotangent), w_qkv, w_out, land_mask, land_bias)
-    return from_quads(att), from_quads(tok), g_qkv, g_out, g_bias[:, 0]
+    )(cells(tokens), cells(cotangent), w_qkv, w_out, land_mask, land_bias)
+    results = (att, tok, g_qkv, g_out, g_bias)
+    att, tok, g_qkv, g_out, g_bias = pl.pallas_call(
+        place,
+        out_shape=[jax.ShapeDtypeStruct(x.shape, x.dtype) for x in results],
+        in_specs=[vmem] * 5,
+        out_specs=[vmem] * 5,
+        compiler_params=pltpu.CompilerParams(vmem_limit_bytes=60 << 20),
+        name="place",
+    )(*results)
+    return levels(att), levels(tok), g_qkv, g_out.T, g_bias.reshape(HEADS)
 
 
 def solution(mesh):

time: 85.5 us -> 68.9 us (0.81)
  the two profiles are of different devices: /device:TPU:6 before, /device:TPU:7 now
where the time goes in v2:
time: 68.9 us; the launch traced here: 68.7 us
  Pallas kernels  68.1 us (99%)
    pallas_call x1, Pallas kernels, shards(): pl.pallas_call(kernel, out_shape=[jax.ShapeDtypeStruct((CELLS, 4, D), BF)...  66.2 us
    pallas_call x1, Pallas kernels, shards(): pl.pallas_call(place, out_shape=[jax.ShapeDtypeStruct(x.shape, x.dtype) f...  1.91 us

profile of v2, /device:TPU:7, one launch (start us, length us, event | category | flops | bytes accessed | tf_op | source)
XLA Modules:
  0.0 68.7 jit_solution(16123023505957381759)
XLA Ops:
  0.6 66.2 %swin_block.1 = (bf16[72,4,512]{2,1,0:T(4,128)(2,1)}, bf16[72,4,512]{2,1,0:T(4,128)(2,1)}, f32[32,48]{1,0:T(8,128)}, f32[16,32]{1,0:T(8,128)}, f32[1,8]{1,0:T(1,128)}) custom-call(bf16[72,4,512]{2,1,0:T(4,128)(2,1)} %bitcast.14, bf16[72,4,512]{2,1,0:T(4,128)(2,1)} %bitcast.15, bf16[512,1536]{1,0:T(8,128)(2,1)} %wqkv_h.1, bf16[512,512]{1,0:T(8,128)(2,1)} %wout_h.1, ...), custom_call_target="tpu_custom_call" | custom-call | tf_op jit(solution)/shard_map/swin_block/pallas_call | solution.py:436
  66.8 1.9 %place.1 = (bf16[72,4,512]{2,1,0:T(4,128)(2,1)}, bf16[72,4,512]{2,1,0:T(4,128)(2,1)}, f32[32,48]{1,0:T(8,128)}, f32[16,32]{1,0:T(8,128)}, f32[1,8]{1,0:T(1,128)}) custom-call(bf16[72,4,512]{2,1,0:T(4,128)(2,1)} %get-tuple-element.15.refs_0_, bf16[72,4,512]{2,1,0:T(4,128)(2,1)} %get-tuple-element.16.refs_1_, f32[32,48]{1,0:T(8,128)} %get-tuple-element.17.refs_2_, ...), custom_call_target="tpu_custom_call" | custom-call | tf_op jit(solution)/shard_map/place/pallas_call | solution.py:482

commit v3 on v2

--- a/solution.py
+++ b/solution.py
@@ -14,7 +14,7 @@
 WIN = 144
 PART = 36
 CELLS = 72
-PADDED = CELLS * 16
+PADDED = CELLS * 8
 QROWS = 80
 NX, NY, NZ = 4, 8, 8
 
@@ -63,16 +63,16 @@
     row = (pos >= 6).astype(jnp.int32) + (pos >= 12).astype(jnp.int32)
     col = pos - 6 * row
     lev = (step + 1) & 3
-    at = ((3 * (1 - (quad & 1)) + row) * 12 + 6 * (1 - (quad >> 1)) + col) * 16 + lev
+    at = ((3 * (1 - (quad & 1)) + row) * 12 + 6 * (1 - (quad >> 1)) + col) * 8 + lev
     return jnp.where(rem < 72, at, -1)
 
 
 def kernel(
     tok_h, cot_h, wqkv_h, wout_h, land, bias,
     out_att, out_tok, g_qkv, g_out, g_bias,
-    tok_v, cot_v, raw, xq, cq, hx, hc, att_q, tok_q, spread,
+    tok_v, cot_v, raw, xq, cq, hx, hc, att_q, tok_q, spread, probs, prob_b, d_prob, d_score, ka, qa,
     wqkv, wout, wt, perm, sel, selt, normal, inv,
-    normw, cotw, nmt, qkvt, dmt, mixt, mixp, dqkvt, r_q, r_o,
+    normw, cotw, nmt, vt, dmt, mixt, mixp, dqkvt, r_q, r_o,
     oa, ot, core_s, core_r,
     a1, ra1, a2, ra2, a3, ra3, b1, rb1, b2, rb2, b3, rb3, c1, rc1, c2, rc2, c3, rc3,
     dbias, bc, bx, by, bz,
@@ -121,13 +121,15 @@
     o_copy = pltpu.make_async_copy(wout_h, wout, lsem.at[1])
     o_copy.start()
     raw[...] = jnp.zeros_like(raw)
-    spread[...] = one_hot(iota((PADDED, 4 * QROWS), 0) == grid_row(iota((1, 4 * QROWS), 1)))
     cut = one_hot(grid_row(iota((4 * QROWS, 1), 0)) == iota((4 * QROWS, PADDED), 1))
-    for copy, held, quads in ((t_copy, tok_v, xq), (c_copy, cot_v, cq)):
+
+    def cut_up(copy, held, quads):
         copy.wait()
-        raw[:, 0:4, :] = held[...]
-        grid = raw[...].reshape(PADDED, D)
+        raw[:, 0:4, :] = held[...].astype(F32)
+        grid = raw[...].reshape(PADDED, D).astype(BF)
         quads[...] = nn(cut, grid).astype(BF).reshape(4, QROWS, D)
+
+    cut_up(t_copy, tok_v, xq)
     pl.semaphore_wait(barrier, len(partners))
 
     def send(src, dst, ssem, rsem, where):
@@ -139,8 +141,9 @@
         return copy
 
     halo_x = [send(xq.at[q], hx.at[q - 1], hs.at[q - 1], hr.at[q - 1], back[q]) for q in (3, 1, 2)]
-    halo_c = [send(cq.at[q], hc.at[q - 1], hs.at[q + 2], hr.at[q + 2], back[q]) for q in (3, 1, 2)]
-
+    cut_up(c_copy, cot_v, cq)
+
+    spread[...] = one_hot(iota((PADDED, 4 * QROWS), 0) == grid_row(iota((1, 4 * QROWS), 1)))
     s_col = iota((2 * WIN, 1), 0)
     sel[...] = one_hot(iota((2 * WIN, 4 * QROWS), 1) == quad_row(s_col))
     for w in range(2):
@@ -157,26 +160,37 @@
     f_i = jnp.where(is_a, a & 15, jnp.where(is_b, 16 + (b & 7), 24 + (b & 7)))
     f_c = jnp.where(half == 0, 1 - core, core)
     perm[...] = one_hot(iota((D, D), 1) == f_zh * 256 + f_x * 64 + f_c * 32 + f_i)
+
+    for copy in halo_x:
+        copy.wait_send()
+    halo_c = [send(cq.at[q], hc.at[q - 1], hs.at[q + 2], hr.at[q + 2], back[q]) for q in (3, 1, 2)]
     r_q[...] = jnp.zeros_like(r_q)
     r_o[...] = jnp.zeros_like(r_o)
 
-    quad, _, row, col = token_place(iota((WIN, 1), 0))
+    quad, _, row, col = token_place(iota((1, WIN), 1))
     l_row = lat * 6 + 3 + (quad & 1) * 3 + row
     l_row = jnp.where(l_row >= 96, l_row - 96, l_row)
     l_col = lon * 12 + 6 + (quad >> 1) * 6 + col
     l_col = jnp.where(l_col >= 384, l_col - 384, l_col)
-    picked = nn(one_hot(iota((WIN, 96), 1) == l_row), land[...].astype(F32).astype(BF))
-    land_key = jnp.sum(jnp.where(iota((WIN, 384), 1) == l_col, picked, 0.0), axis=1, keepdims=True)
-
-    def region(t, w):
-        quad, lev, _, _ = token_place(t)
-        seam = jnp.where(lat == 15, 2, 0)
-        return seam * (quad & 1) + (lev if w == 1 else 0)
-
-    masks = [
-        jnp.where(region(iota((WIN, 1), 0), w) == region(iota((1, WIN), 1), w), 0.0, -1e30)
-        for w in range(2)
-    ]
+    picked = nn(land[...].astype(F32).astype(BF), one_hot(iota((384, WIN), 0) == l_col))
+    land_key = jnp.sum(jnp.where(iota((96, WIN), 0) == l_row, picked, 0.0), axis=0, keepdims=True)
+
+    extra = iota((16, WIN), 0)
+    is_land = (extra >= 4) & (extra < 7)
+    for w in range(2):
+        quad, lev, _, _ = token_place(iota((16, WIN), 1))
+        region = jnp.where(lat == 15, 2, 0) * (quad & 1) + (lev if w == 1 else 0)
+        here = extra == region
+        under_keys = jnp.where(here, 1.0, jnp.where(is_land, land_key, 0.0)).astype(BF)
+        barred = jnp.where(here | (extra >= 4), 0.0, -1e30)
+        for h in range(HEADS):
+            full = jnp.zeros((16, WIN), F32) + bias[h]
+            first = full.astype(BF).astype(F32)
+            second = (full - first).astype(BF).astype(F32)
+            third = full - first - second
+            pieces = jnp.where(extra == 4, first, jnp.where(extra == 5, second, third))
+            ka[w, h, HD : HD + 16] = under_keys
+            qa[w, h, HD : HD + 16] = jnp.where(is_land, pieces, barred).astype(BF)
 
     w_copy.wait()
     o_copy.wait()
@@ -193,14 +207,48 @@
 
     layer_norm(xq[0], 0)
     for copy, q in zip(halo_x, (3, 1, 2)):
-        copy.wait()
+        copy.wait_recv()
         layer_norm(hx[q - 1], q)
     normed = normal[...].reshape(4 * QROWS, D).astype(BF)
     normw[...] = nn(sel[...], normed).astype(BF)
     for w in range(2):
         nw = normw[WIN * w : WIN * w + WIN]
-        qkvt[w] = nt(wt[...], nw).astype(BF)
+        qkv = nt(wt[...], nw).astype(BF)
+        for h in range(HEADS):
+            qa[w, h, 0:HD] = qkv[h * HD : h * HD + HD] * (HD ** -0.5)
+            ka[w, h, 0:HD] = qkv[D + h * HD : D + h * HD + HD]
+        vt[w] = qkv[2 * D :]
         nmt[w] = nt(perm[...], nw).astype(BF)
+    pairs = [(w, h) for h in range(HEADS) for w in range(2)]
+
+    def head(h):
+        return slice(h * HD, h * HD + HD)
+
+    for w, h in pairs:
+        probs[w, h] = tn(ka[w, h], qa[w, h])
+    for w, h in pairs:
+        score = probs[w, h]
+        expo = jnp.exp(score - jnp.max(score, axis=0, keepdims=True))
+        prob = expo * (1.0 / jnp.sum(expo, axis=0, keepdims=True))
+        probs[w, h] = prob
+        prob_b[w, h] = prob.astype(BF)
+    for w, h in pairs:
+        mixt[w, head(h)] = nn(vt[w, head(h)], prob_b[w, h]).astype(BF)
+
+    out_sends = []
+
+    def give(q, value, mine, away, far, k):
+        if q == 0:
+            mine[0] = value
+        else:
+            away[q - 1] = value
+            out_sends.append(send(away.at[q - 1], far.at[q], os.at[k], orr.at[k], ahead[q]))
+
+    for q in (3, 1, 2, 0):
+        rows = slice(QROWS * q, QROWS * q + QROWS)
+        mixed = (nt(selt[0, rows], mixt[0]) + nt(selt[1, rows], mixt[1])).astype(BF)
+        give(q, nn(mixed, wout[...]).astype(BF), att_q, oa, att_q, q - 1)
+
     for copy in halo_c:
         copy.wait()
     cot = jnp.concatenate([cq[0], hc[0], hc[1], hc[2]], axis=0)
@@ -214,39 +262,29 @@
                 at = 64 * (16 * k + g) + 48
                 r_o[w, at : at + 16] = ct[16 * g : 16 * g + 16]
 
-    def one_head(h):
-        base = h * HD
-        bias_h = bias[h]
-        d_bias = jnp.zeros((1, WIN), F32)
-        for w in range(2):
-            qt = qkvt[w, pl.ds(base, HD)]
-            kt = qkvt[w, pl.ds(D + base, HD)]
-            vt = qkvt[w, pl.ds(2 * D + base, HD)]
-            dm = dmt[w, pl.ds(base, HD)]
-            score = tn(kt, qt) * (HD ** -0.5) + (bias_h * land_key + masks[w])
-            expo = jnp.exp(score - jnp.max(score, axis=0, keepdims=True))
-            prob = expo * (1.0 / jnp.sum(expo, axis=0, keepdims=True))
-            prob_b = prob.astype(BF)
-            mixt[w, pl.ds(base, HD)] = nn(vt, prob_b).astype(BF)
-            d_prob = tn(vt, dm).astype(BF).astype(F32)
-            d_v = nt(dm, prob_b).astype(BF)
-            d_score = prob * (d_prob - jnp.sum(prob * d_prob, axis=0, keepdims=True))
-            d_bias = d_bias + jnp.sum(d_score * land_key, axis=0, keepdims=True)
-            ds_b = d_score.astype(BF)
-            d_q = (nn(kt, ds_b) * (HD ** -0.5)).astype(BF)
-            d_k = (nt(qt, ds_b) * (HD ** -0.5)).astype(BF)
-            for part, grad in enumerate((d_q, d_k, d_v)):
-                dqkvt[w, pl.ds(part * D + base, HD)] = grad
-                for g in range(4):
-                    piece = h * 4 + (part * 32 + g)
-                    at = (piece // 3) * 64 + (piece % 3) * 16
-                    r_q[w, pl.ds(at, 16)] = grad[16 * g : 16 * g + 16]
-        dbias[h : h + 1] = d_bias
-
-    for h in range(HEADS):
-        one_head(h)
-
-    bc[0] = jnp.broadcast_to(jnp.sum(dbias[...], axis=1, keepdims=True), (HEADS, 128))
+    for w, h in pairs:
+        d_prob[w, h] = tn(vt[w, head(h)], dmt[w, head(h)]).astype(BF)
+
+    def keep(w, h, k, grad):
+        dqkvt[w, k * D + h * HD : k * D + h * HD + HD] = grad
+        for g in range(4):
+            piece = h * 4 + k * 32 + g
+            at = (piece // 3) * 64 + (piece % 3) * 16
+            r_q[w, at : at + 16] = grad[16 * g : 16 * g + 16]
+
+    for w, h in pairs:
+        keep(w, h, 2, nt(dmt[w, head(h)], prob_b[w, h]).astype(BF))
+    for w, h in pairs:
+        prob = probs[w, h]
+        dp = d_prob[w, h].astype(F32)
+        d_score[w, h] = (prob * (dp - jnp.sum(prob * dp, axis=0, keepdims=True))).astype(BF)
+    for w, h in pairs:
+        under = nn(ka[w, h], d_score[w, h])
+        keep(w, h, 0, (under[0:HD] * (HD ** -0.5)).astype(BF))
+        dbias[w, h : h + 1] = under[HD + 4 : HD + 5]
+        keep(w, h, 1, nt(qa[w, h, 0:HD], d_score[w, h]).astype(BF))
+
+    bc[0] = jnp.broadcast_to(jnp.sum(dbias[0] + dbias[1], axis=1, keepdims=True), (HEADS, 128))
     bias_c = send(bc.at[0], bc.at[1], cs.at[0], cr.at[0], at_core())
 
     for w in range(2):
@@ -267,20 +305,6 @@
         if y % 2 == 1:
             pair, k = slice(y - 1, y + 1), 1 + y // 2
             core_copies.append(send(core_s.at[pair], core_r.at[pair], cs.at[k], cr.at[k], at_core()))
-
-    out_sends = []
-
-    def give(q, value, mine, away, far, k):
-        if q == 0:
-            mine[0] = value
-        else:
-            away[q - 1] = value
-            out_sends.append(send(away.at[q - 1], far.at[q], os.at[k], orr.at[k], ahead[q]))
-
-    for q in (3, 1, 2, 0):
-        rows = slice(QROWS * q, QROWS * q + QROWS)
-        mixed = (nt(selt[0, rows], mixt[0]) + nt(selt[1, rows], mixt[1])).astype(BF)
-        give(q, nn(mixed, wout[...]).astype(BF), att_q, oa, att_q, q - 1)
 
     lane_low = iota((64, 128), 1) < 64
     kept = []
@@ -323,9 +347,9 @@
             total = total + parts[d].astype(F32)
         return total
 
+    go_a = swap_x(lambda d: a1.at[(px + d) & 3], ra1, 0)
+    go_b = swap_y(lambda d: b1.at[(py + d) & 7], rb1, 0)
     go_c = swap_z(lambda d: c1.at[(pz + d) & 7], rc1, 0)
-    go_b = swap_y(lambda d: b1.at[(py + d) & 7], rb1, 0)
-    go_a = swap_x(lambda d: a1.at[(px + d) & 3], ra1, 0)
     bias_c.wait()
     bx[0] = bc[0] + bc[1]
     go_bias = [send(bx.at[0], bx.at[d], xs.at[3, d - 1], xr.at[3, d - 1], at_x(d)) for d in (2, 1, 3)]
@@ -371,6 +395,13 @@
     by[0] = ordered(bx, px, NX)
     go_bias = [send(by.at[0], by.at[d], ys.at[3, d - 1], yr.at[3, d - 1], at_y(d)) for d in (4, 3, 5, 2, 6, 1, 7)]
 
+    def to_grid(quads, out):
+        grid = nn(spread[...], quads[...].reshape(4 * QROWS, D))
+        out[...] = grid.reshape(CELLS, 8, D)[:, 0:4, :].astype(BF)
+
+    wait(out_sends[:3])
+    to_grid(att_q, out_att)
+
     wait(go_a)
     total = summed(a2[py], ra2, 7)
     for zh in range(2):
@@ -394,10 +425,8 @@
     def mine(total, odd):
         return jnp.where(odd == 1, pltpu.roll(total, 64, 1), total)
 
-    wait(out_sends)
-    for quads, out in ((att_q, out_att), (tok_q, out_tok)):
-        grid = nn(spread[...], quads[...].reshape(4 * QROWS, D)).astype(BF)
-        out[...] = grid.reshape(CELLS, 16, D)[:, 0:4, :]
+    wait(out_sends[3:])
+    to_grid(tok_q, out_tok)
 
     wait(go_a)
     grad_a = mine(summed(a3[pz >> 1], ra3, 7), pzl & 1)
@@ -415,9 +444,18 @@
 
 
 def place(*refs):
-    count = len(refs) // 2
+    count = (len(refs) - 2) // 3
+    src, dst, held = refs[:count], refs[count : 2 * count], refs[2 * count : 3 * count]
+    came, went = refs[-2:]
+    into = [pltpu.make_async_copy(src[k], held[k], came.at[k]) for k in range(count)]
+    out = [pltpu.make_async_copy(held[k], dst[k], went.at[k]) for k in range(count)]
+    for copy in into:
+        copy.start()
     for k in range(count):
-        refs[count + k][...] = refs[k][...]
+        into[k].wait()
+        out[k].start()
+    for copy in out:
+        copy.wait()
 
 
 def cells(grid):
@@ -445,15 +483,18 @@
         in_specs=[anywhere, anywhere, anywhere, anywhere, vmem, pl.BlockSpec(memory_space=pltpu.SMEM)],
         out_specs=[vmem] * 5,
         scratch_shapes=[
-            V((CELLS, 4, D), BF), V((CELLS, 4, D), BF), V((CELLS, 16, D), BF),
+            V((CELLS, 4, D), BF), V((CELLS, 4, D), BF), V((CELLS, 8, D), F32),
             V((4, QROWS, D), BF), V((4, QROWS, D), BF),
             V((3, QROWS, D), BF), V((3, QROWS, D), BF),
             V((4, QROWS, D), BF), V((4, QROWS, D), BF), V((PADDED, 4 * QROWS), BF),
+            V((2, HEADS, WIN, WIN), F32), V((2, HEADS, WIN, WIN), BF),
+            V((2, HEADS, WIN, WIN), BF), V((2, HEADS, WIN, WIN), BF),
+            V((2, HEADS, HD + 16, WIN), BF), V((2, HEADS, HD + 16, WIN), BF),
             V((D, 3 * D), BF), V((D, D), BF), V((3 * D, D), BF),
             V((D, D), BF), V((2 * WIN, 4 * QROWS), BF), V((2, 4 * QROWS, WIN), BF),
             V((4, QROWS, D), F32), V((4, QROWS, 128), F32),
             V((2 * WIN, D), BF), V((2 * WIN, D), BF),
-            V((2, D, WIN), BF), V((2, 3 * D, WIN), BF), V((2, D, WIN), BF),
+            V((2, D, WIN), BF), V((2, D, WIN), BF), V((2, D, WIN), BF),
             V((2, D, WIN), BF), V((2, D, WIN), BF), V((2, 3 * D, WIN), BF),
             V((2, 4 * D, WIN), BF), V((2, 4 * D, WIN), BF),
             V((3, QROWS, D), BF), V((3, QROWS, D), BF),
@@ -467,7 +508,7 @@
             V((NZ, 32, 512), BF), V((7, 32, 512), BF),
             V((NX, 8, 512), F32), V((3, 8, 512), F32),
             V((4, 8, 128), F32), V((7, 8, 128), F32),
-            V((HEADS, WIN), F32), V((2, HEADS, 128), F32),
+            V((2, HEADS, WIN), F32), V((2, HEADS, 128), F32),
             V((NX, HEADS, 128), F32), V((NY, HEADS, 128), F32), V((NZ, HEADS, 128), F32),
             dma((4,)), dma((6,)), dma((6,)), dma((6,)), dma((6,)),
             dma((5,)), dma((5,)),
@@ -482,8 +523,9 @@
     att, tok, g_qkv, g_out, g_bias = pl.pallas_call(
         place,
         out_shape=[jax.ShapeDtypeStruct(x.shape, x.dtype) for x in results],
-        in_specs=[vmem] * 5,
-        out_specs=[vmem] * 5,
+        in_specs=[anywhere] * 5,
+        out_specs=[anywhere] * 5,
+        scratch_shapes=[V(x.shape, x.dtype) for x in results] + [dma((5,)), dma((5,))],
         compiler_params=pltpu.CompilerParams(vmem_limit_bytes=60 << 20),
         name="place",
     )(*results)

time: 68.9 us -> 64.4 us (0.935)
  the two profiles are of different devices: /device:TPU:7 before, /device:TPU:6 now
where the time goes in v3:
time: 64.4 us; the launch traced here: 64.2 us
  Pallas kernels  63.5 us (99%)
    pallas_call x1, Pallas kernels, shards(): pl.pallas_call(kernel, out_shape=[jax.ShapeDtypeStruct((CELLS, 4, D), BF)...  61.7 us
    pallas_call x1, Pallas kernels, shards(): pl.pallas_call(place, out_shape=[jax.ShapeDtypeStruct(x.shape, x.dtype) f...  1.87 us

profile of v3, /device:TPU:6, one launch (start us, length us, event | category | flops | bytes accessed | tf_op | source)
XLA Modules:
  0.0 64.2 jit_solution(11032287554859493198)
XLA Ops:
  0.6 61.7 %swin_block.1 = (bf16[72,4,512]{2,1,0:T(4,128)(2,1)}, bf16[72,4,512]{2,1,0:T(4,128)(2,1)}, f32[32,48]{1,0:T(8,128)}, f32[16,32]{1,0:T(8,128)}, f32[1,8]{1,0:T(1,128)}) custom-call(bf16[72,4,512]{2,1,0:T(4,128)(2,1)} %bitcast.14, bf16[72,4,512]{2,1,0:T(4,128)(2,1)} %bitcast.15, bf16[512,1536]{1,0:T(8,128)(2,1)} %wqkv_h.1, bf16[512,512]{1,0:T(8,128)(2,1)} %wout_h.1, ...), custom_call_target="tpu_custom_call" | custom-call | tf_op jit(solution)/shard_map/swin_block/pallas_call | solution.py:474
  62.3 1.9 %place.1 = (bf16[72,4,512]{2,1,0:T(4,128)(2,1)}, bf16[72,4,512]{2,1,0:T(4,128)(2,1)}, f32[32,48]{1,0:T(8,128)}, f32[16,32]{1,0:T(8,128)}, f32[1,8]{1,0:T(1,128)}) custom-call(bf16[72,4,512]{2,1,0:T(4,128)(2,1)} %get-tuple-element.15.refs_0_, bf16[72,4,512]{2,1,0:T(4,128)(2,1)} %get-tuple-element.16.refs_1_, f32[32,48]{1,0:T(8,128)} %get-tuple-element.17.refs_2_, ...), custom_call_target="tpu_custom_call" | custom-call | tf_op jit(solution)/shard_map/place/pallas_call | solution.py:523

commit v4 on v3

--- a/solution.py
+++ b/solution.py
@@ -12,10 +12,7 @@
 HEADS = 8
 HD = 64
 WIN = 144
-PART = 36
-CELLS = 72
-PADDED = CELLS * 8
-QROWS = 80
+QROWS = 18 * 8
 NX, NY, NZ = 4, 8, 8
 
 
@@ -50,27 +47,14 @@
 
 def quad_row(s):
     w = (s >= WIN).astype(jnp.int32)
-    t = s - WIN * w
-    quad = (t >= 36).astype(jnp.int32) + (t >= 72).astype(jnp.int32) + (t >= 108).astype(jnp.int32)
-    return quad * QROWS + w * PART + (t - 36 * quad)
-
-
-def grid_row(s):
-    quad = (s >= QROWS).astype(jnp.int32) + (s >= 2 * QROWS).astype(jnp.int32) + (s >= 3 * QROWS).astype(jnp.int32)
-    rem = s - QROWS * quad
-    step = (rem >= 18).astype(jnp.int32) + (rem >= 36).astype(jnp.int32) + (rem >= 54).astype(jnp.int32)
-    pos = rem - 18 * step
-    row = (pos >= 6).astype(jnp.int32) + (pos >= 12).astype(jnp.int32)
-    col = pos - 6 * row
-    lev = (step + 1) & 3
-    at = ((3 * (1 - (quad & 1)) + row) * 12 + 6 * (1 - (quad >> 1)) + col) * 8 + lev
-    return jnp.where(rem < 72, at, -1)
+    quad, lev, row, col = token_place(s - WIN * w)
+    return quad * QROWS + (row * 6 + col) * 8 + ((2 * w + lev + 1) & 3)
 
 
 def kernel(
     tok_h, cot_h, wqkv_h, wout_h, land, bias,
     out_att, out_tok, g_qkv, g_out, g_bias,
-    tok_v, cot_v, raw, xq, cq, hx, hc, att_q, tok_q, spread, probs, prob_b, d_prob, d_score, ka, qa,
+    tok_v, cot_v, padded, hx, hc, probs, prob_b, d_prob, d_score, ka, qa,
     wqkv, wout, wt, perm, sel, selt, normal, inv,
     normw, cotw, nmt, vt, dmt, mixt, mixp, dqkvt, r_q, r_o,
     oa, ot, core_s, core_r,
@@ -120,16 +104,8 @@
     w_copy.start()
     o_copy = pltpu.make_async_copy(wout_h, wout, lsem.at[1])
     o_copy.start()
-    raw[...] = jnp.zeros_like(raw)
-    cut = one_hot(grid_row(iota((4 * QROWS, 1), 0)) == iota((4 * QROWS, PADDED), 1))
-
-    def cut_up(copy, held, quads):
-        copy.wait()
-        raw[:, 0:4, :] = held[...].astype(F32)
-        grid = raw[...].reshape(PADDED, D).astype(BF)
-        quads[...] = nn(cut, grid).astype(BF).reshape(4, QROWS, D)
-
-    cut_up(t_copy, tok_v, xq)
+    t_copy.wait()
+    c_copy.wait()
     pl.semaphore_wait(barrier, len(partners))
 
     def send(src, dst, ssem, rsem, where):
@@ -140,10 +116,18 @@
         copy.start()
         return copy
 
-    halo_x = [send(xq.at[q], hx.at[q - 1], hs.at[q - 1], hr.at[q - 1], back[q]) for q in (3, 1, 2)]
-    cut_up(c_copy, cot_v, cq)
-
-    spread[...] = one_hot(iota((PADDED, 4 * QROWS), 0) == grid_row(iota((1, 4 * QROWS), 1)))
+    places = [(slice(3 - 3 * (q & 1), 6 - 3 * (q & 1)), slice(6 - 6 * (q >> 1), 12 - 6 * (q >> 1))) for q in range(4)]
+
+    def halo(held, far, first):
+        return [
+            send(held.at[places[q]], far.at[q - 1], hs.at[first + q - 1], hr.at[first + q - 1], back[q])
+            for q in (3, 1, 2)
+        ]
+
+    halo_x = halo(tok_v, hx, 0)
+    halo_c = halo(cot_v, hc, 3)
+
+    padded[...] = jnp.zeros_like(padded)
     s_col = iota((2 * WIN, 1), 0)
     sel[...] = one_hot(iota((2 * WIN, 4 * QROWS), 1) == quad_row(s_col))
     for w in range(2):
@@ -161,9 +145,6 @@
     f_c = jnp.where(half == 0, 1 - core, core)
     perm[...] = one_hot(iota((D, D), 1) == f_zh * 256 + f_x * 64 + f_c * 32 + f_i)
 
-    for copy in halo_x:
-        copy.wait_send()
-    halo_c = [send(cq.at[q], hc.at[q - 1], hs.at[q + 2], hr.at[q + 2], back[q]) for q in (3, 1, 2)]
     r_q[...] = jnp.zeros_like(r_q)
     r_o[...] = jnp.zeros_like(r_o)
 
@@ -198,19 +179,19 @@
     for k in range(6):
         wt[256 * k : 256 * k + 256] = nt(eye, wqkv[:, 256 * k : 256 * k + 256]).astype(BF)
 
-    def layer_norm(x, q):
-        x = x.astype(F32)
-        centred = x - jnp.mean(x, axis=1, keepdims=True)
-        scale = lax.rsqrt(jnp.mean(centred * centred, axis=1, keepdims=True) + 1e-05)
-        normal[q] = centred * scale
-        inv[q] = jnp.broadcast_to(scale, (QROWS, 128))
-
-    layer_norm(xq[0], 0)
-    for copy, q in zip(halo_x, (3, 1, 2)):
-        copy.wait_recv()
-        layer_norm(hx[q - 1], q)
-    normed = normal[...].reshape(4 * QROWS, D).astype(BF)
-    normw[...] = nn(sel[...], normed).astype(BF)
+    def gather(own, far, copies):
+        padded[0, :, 0:4] = own[places[0]].reshape(18, 4, D).astype(F32)
+        for copy, q in zip(copies, (3, 1, 2)):
+            copy.wait()
+            padded[q, :, 0:4] = far[q - 1].reshape(18, 4, D).astype(F32)
+        return nn(sel[...], padded[...].reshape(4 * QROWS, D).astype(BF))
+
+    x = gather(tok_v, hx, halo_x)
+    centred = x - jnp.mean(x, axis=1, keepdims=True)
+    scale = lax.rsqrt(jnp.mean(centred * centred, axis=1, keepdims=True) + 1e-05)
+    normal[...] = centred * scale
+    inv[...] = jnp.broadcast_to(scale, (2 * WIN, 128))
+    normw[...] = normal[...].astype(BF)
     for w in range(2):
         nw = normw[WIN * w : WIN * w + WIN]
         qkv = nt(wt[...], nw).astype(BF)
@@ -237,22 +218,20 @@
 
     out_sends = []
 
-    def give(q, value, mine, away, far, k):
+    def give(q, value, away, far, k):
+        value = value.reshape(18, 8, D)[:, 0:4].reshape(3, 6, 4, D).astype(BF)
         if q == 0:
-            mine[0] = value
+            far[places[0]] = value
         else:
             away[q - 1] = value
-            out_sends.append(send(away.at[q - 1], far.at[q], os.at[k], orr.at[k], ahead[q]))
+            out_sends.append(send(away.at[q - 1], far.at[places[q]], os.at[k], orr.at[k], ahead[q]))
 
     for q in (3, 1, 2, 0):
         rows = slice(QROWS * q, QROWS * q + QROWS)
         mixed = (nt(selt[0, rows], mixt[0]) + nt(selt[1, rows], mixt[1])).astype(BF)
-        give(q, nn(mixed, wout[...]).astype(BF), att_q, oa, att_q, q - 1)
-
-    for copy in halo_c:
-        copy.wait()
-    cot = jnp.concatenate([cq[0], hc[0], hc[1], hc[2]], axis=0)
-    cotw[...] = nn(sel[...], cot).astype(BF)
+        give(q, nn(mixed, wout[...]), oa, out_att, q - 1)
+
+    cotw[...] = gather(cot_v, hc, halo_c).astype(BF)
     for w in range(2):
         cw = cotw[WIN * w : WIN * w + WIN]
         dmt[w] = nt(wout[...], cw).astype(BF)
@@ -354,16 +333,29 @@
     bx[0] = bc[0] + bc[1]
     go_bias = [send(bx.at[0], bx.at[d], xs.at[3, d - 1], xr.at[3, d - 1], at_x(d)) for d in (2, 1, 3)]
 
+    eye_w = one_hot(iota((WIN, WIN), 0) == iota((WIN, WIN), 1))
+    d_tok = []
+    for w in range(2):
+        d_qkv = nt(eye_w, dqkvt[w]).astype(BF)
+        d_normed = nn(d_qkv, wt[...])
+        norm = normal[WIN * w : WIN * w + WIN]
+        mean_grad = jnp.mean(d_normed, axis=1, keepdims=True)
+        mean_cross = jnp.mean(d_normed * norm, axis=1, keepdims=True)
+        d_x = inv[WIN * w : WIN * w + WIN, 0:1] * (d_normed - mean_grad - norm * mean_cross)
+        d_tok.append(d_x.astype(BF))
     for q in (3, 1, 2, 0):
         rows = slice(QROWS * q, QROWS * q + QROWS)
-        d_qkv = (nt(selt[0, rows], dqkvt[0]) + nt(selt[1, rows], dqkvt[1])).astype(BF)
-        d_normed = nn(d_qkv, wt[...])
-        norm = normal[q]
-        mean_grad = jnp.mean(d_normed, axis=1, keepdims=True)
-        mean_cross = jnp.mean(d_normed * norm, axis=1, keepdims=True)
-        d_tok = (inv[q][:, 0:1] * (d_normed - mean_grad - norm * mean_cross)).astype(BF)
-        give(q, d_tok, tok_q, ot, tok_q, q + 2)
-
+        give(q, nn(selt[0, rows], d_tok[0]) + nn(selt[1, rows], d_tok[1]), ot, out_tok, q + 2)
+
+    def ordered(slots, me, n):
+        total = slots[me & (n - 1)]
+        for k in range(1, n):
+            total = total + slots[(me - k) & (n - 1)]
+        return total
+
+    wait(go_bias)
+    by[0] = ordered(bx, px, NX)
+    go_bias = [send(by.at[0], by.at[d], ys.at[3, d - 1], yr.at[3, d - 1], at_y(d)) for d in (4, 3, 5, 2, 6, 1, 7)]
     wait(go_a)
     for y in range(NY):
         total = a1[px, y].astype(F32)
@@ -384,63 +376,44 @@
     for x in range(NX):
         c2[x] = total[8 * x : 8 * x + 8]
     go_c = swap_x(lambda d: c2.at[(px + d) & 3], rc2, 1)
+
     wait(go_bias)
-
-    def ordered(slots, me, n):
-        total = slots[me & (n - 1)]
-        for k in range(1, n):
-            total = total + slots[(me - k) & (n - 1)]
-        return total
-
-    by[0] = ordered(bx, px, NX)
-    go_bias = [send(by.at[0], by.at[d], ys.at[3, d - 1], yr.at[3, d - 1], at_y(d)) for d in (4, 3, 5, 2, 6, 1, 7)]
-
-    def to_grid(quads, out):
-        grid = nn(spread[...], quads[...].reshape(4 * QROWS, D))
-        out[...] = grid.reshape(CELLS, 8, D)[:, 0:4, :].astype(BF)
-
-    wait(out_sends[:3])
-    to_grid(att_q, out_att)
-
+    bz[0] = ordered(by, py, NY)
+    go_bias = [send(bz.at[0], bz.at[d], zs.at[3, d - 1], zr.at[3, d - 1], at_z(d)) for d in (4, 3, 5, 2, 6, 1, 7)]
+    wait(go_c)
+    total = summed(c2[px], rc2, 3)
+    for m in range(4):
+        c3[m] = total[:, 128 * m : 128 * m + 128]
+    go_c = swap_y(lambda d: c3.at[((py + d) & 7) >> 1], rc3, 2)
+    wait(go_b)
+    total = summed(b2[pz >> 1], rb2, 7)
+    for x in range(NX):
+        b3[x] = total[8 * x : 8 * x + 8]
+    go_b = swap_x(lambda d: b3.at[(px + d) & 3], rb3, 2)
     wait(go_a)
     total = summed(a2[py], ra2, 7)
     for zh in range(2):
         for t in range(2):
             a3[zh * 2 + t] = total[16 * zh : 16 * zh + 16, 128 * t : 128 * t + 128]
     go_a = swap_z(lambda d: a3.at[((pz + d) & 7) >> 1], ra3, 2)
-    wait(go_b)
-    total = summed(b2[pz >> 1], rb2, 7)
-    for x in range(NX):
-        b3[x] = total[8 * x : 8 * x + 8]
-    go_b = swap_x(lambda d: b3.at[(px + d) & 3], rb3, 2)
-    wait(go_c)
-    total = summed(c2[px], rc2, 3)
-    for m in range(4):
-        c3[m] = total[:, 128 * m : 128 * m + 128]
-    go_c = swap_y(lambda d: c3.at[((py + d) & 7) >> 1], rc3, 2)
-    wait(go_bias)
-    bz[0] = ordered(by, py, NY)
-    go_bias = [send(bz.at[0], bz.at[d], zs.at[3, d - 1], zr.at[3, d - 1], at_z(d)) for d in (4, 3, 5, 2, 6, 1, 7)]
 
     def mine(total, odd):
         return jnp.where(odd == 1, pltpu.roll(total, 64, 1), total)
 
-    wait(out_sends[3:])
-    to_grid(tok_q, out_tok)
-
-    wait(go_a)
-    grad_a = mine(summed(a3[pz >> 1], ra3, 7), pzl & 1)
+    wait(go_bias)
+    total = ordered(bz, pz, NZ)
+    on_diagonal = iota((HEADS, 128), 0) == iota((HEADS, 128), 1)
+    g_bias[...] = jnp.sum(jnp.where(on_diagonal, total, 0.0), axis=0, keepdims=True)[:, 0:HEADS]
+    wait(out_sends)
     wait(go_b)
     grad_b = mine(summed(b3[px], rb3, 3), pzl & 1)
     wait(go_c)
     grad_c = mine(summed(c3[py >> 1], rc3, 7), py & 1)
+    wait(go_a)
+    grad_a = mine(summed(a3[pz >> 1], ra3, 7), pzl & 1)
     grads = jnp.concatenate([grad_a, grad_b, grad_c], axis=0)
     g_qkv[...] = grads[:, 0:48]
     g_out[...] = grads.T[48:64]
-    wait(go_bias)
-    total = ordered(bz, pz, NZ)
-    on_diagonal = iota((HEADS, 128), 0) == iota((HEADS, 128), 1)
-    g_bias[...] = jnp.sum(jnp.where(on_diagonal, total, 0.0), axis=0, keepdims=True)[:, 0:HEADS]
 
 
 def place(*refs):
@@ -459,11 +432,11 @@
 
 
 def cells(grid):
-    return grid.transpose(1, 2, 0, 3).reshape(CELLS, 4, D)
+    return grid.transpose(1, 2, 0, 3)
 
 
 def levels(grid):
-    return grid.reshape(6, 12, 4, D).transpose(2, 0, 1, 3)
+    return grid.transpose(2, 0, 1, 3)
 
 
 def shards(tokens, cotangent, w_qkv, w_out, land_mask, land_bias):
@@ -474,8 +447,8 @@
     att, tok, g_qkv, g_out, g_bias = pl.pallas_call(
         kernel,
         out_shape=[
-            jax.ShapeDtypeStruct((CELLS, 4, D), BF),
-            jax.ShapeDtypeStruct((CELLS, 4, D), BF),
+            jax.ShapeDtypeStruct((6, 12, 4, D), BF),
+            jax.ShapeDtypeStruct((6, 12, 4, D), BF),
             jax.ShapeDtypeStruct((32, 48), F32),
             jax.ShapeDtypeStruct((16, 32), F32),
             jax.ShapeDtypeStruct((1, HEADS), F32),
@@ -483,21 +456,19 @@
         in_specs=[anywhere, anywhere, anywhere, anywhere, vmem, pl.BlockSpec(memory_space=pltpu.SMEM)],
         out_specs=[vmem] * 5,
         scratch_shapes=[
-            V((CELLS, 4, D), BF), V((CELLS, 4, D), BF), V((CELLS, 8, D), F32),
-            V((4, QROWS, D), BF), V((4, QROWS, D), BF),
-            V((3, QROWS, D), BF), V((3, QROWS, D), BF),
-            V((4, QROWS, D), BF), V((4, QROWS, D), BF), V((PADDED, 4 * QROWS), BF),
+            V((6, 12, 4, D), BF), V((6, 12, 4, D), BF), V((4, 18, 8, D), F32),
+            V((3, 3, 6, 4, D), BF), V((3, 3, 6, 4, D), BF),
             V((2, HEADS, WIN, WIN), F32), V((2, HEADS, WIN, WIN), BF),
             V((2, HEADS, WIN, WIN), BF), V((2, HEADS, WIN, WIN), BF),
             V((2, HEADS, HD + 16, WIN), BF), V((2, HEADS, HD + 16, WIN), BF),
             V((D, 3 * D), BF), V((D, D), BF), V((3 * D, D), BF),
             V((D, D), BF), V((2 * WIN, 4 * QROWS), BF), V((2, 4 * QROWS, WIN), BF),
-            V((4, QROWS, D), F32), V((4, QROWS, 128), F32),
+            V((2 * WIN, D), F32), V((2 * WIN, 128), F32),
             V((2 * WIN, D), BF), V((2 * WIN, D), BF),
             V((2, D, WIN), BF), V((2, D, WIN), BF), V((2, D, WIN), BF),
             V((2, D, WIN), BF), V((2, D, WIN), BF), V((2, 3 * D, WIN), BF),
             V((2, 4 * D, WIN), BF), V((2, 4 * D, WIN), BF),
-            V((3, QROWS, D), BF), V((3, QROWS, D), BF),
+            V((3, 3, 6, 4, D), BF), V((3, 3, 6, 4, D), BF),
             V((NY, 256, 256), BF), V((NY, 256, 256), BF),
             V((NX, NY, 32, 256), BF), V((3, NY, 32, 256), BF),
             V((NY, 32, 256), BF), V((7, 32, 256), BF),

time: 64.4 us -> 62.6 us (0.972); the launches traced: 64.2 us -> 61.4 us
  Pallas kernels: 63.5 us -> 60.7 us
    pallas_call x1, Pallas kernels: 61.7 us -> 58.9 us  [shards(): pl.pallas_call(kernel, out_shape=[jax.ShapeDtypeStruct((6, 12, 4, D), BF)...]
where the time goes in v4:
time: 62.6 us; the launch traced here: 61.4 us
  Pallas kernels  60.7 us (97%)
  between operations  0.64 us (1%)
    pallas_call x1, Pallas kernels, shards(): pl.pallas_call(kernel, out_shape=[jax.ShapeDtypeStruct((6, 12, 4, D), BF)...  58.9 us
    pallas_call x1, Pallas kernels, shards(): pl.pallas_call(place, out_shape=[jax.ShapeDtypeStruct(x.shape, x.dtype) f...  1.87 us

profile of v4, /device:TPU:6, one launch (start us, length us, event | category | flops | bytes accessed | tf_op | source)
XLA Modules:
  0.0 61.4 jit_solution(4400454087797429454)
XLA Ops:
  0.6 58.9 %swin_block.1 = (bf16[6,12,4,512]{3,2,1,0:T(4,128)(2,1)}, bf16[6,12,4,512]{3,2,1,0:T(4,128)(2,1)}, f32[32,48]{1,0:T(8,128)}, f32[16,32]{1,0:T(8,128)}, f32[1,8]{1,0:T(1,128)}) custom-call(bf16[6,12,4,512]{3,2,1,0:T(4,128)(2,1)} %bitcast.6, bf16[6,12,4,512]{3,2,1,0:T(4,128)(2,1)} %bitcast.7, bf16[512,1536]{1,0:T(8,128)(2,1)} %wqkv_h.1, ...), custom_call_target="tpu_custom_call" | custom-call | tf_op jit(solution)/shard_map/swin_block/pallas_call | solution.py:447
  59.5 1.9 %place.1 = (bf16[6,12,4,512]{3,2,1,0:T(4,128)(2,1)}, bf16[6,12,4,512]{3,2,1,0:T(4,128)(2,1)}, f32[32,48]{1,0:T(8,128)}, f32[16,32]{1,0:T(8,128)}, f32[1,8]{1,0:T(1,128)}) custom-call(bf16[6,12,4,512]{3,2,1,0:T(4,128)(2,1)} %get-tuple-element.15.refs_0_, bf16[6,12,4,512]{3,2,1,0:T(4,128)(2,1)} %get-tuple-element.16.refs_1_, ...), custom_call_target="tpu_custom_call" | custom-call | tf_op jit(solution)/shard_map/place/pallas_call | solution.py:494

commit v5 on v4

--- a/solution.py
+++ b/solution.py
@@ -57,7 +57,7 @@
     tok_v, cot_v, padded, hx, hc, probs, prob_b, d_prob, d_score, ka, qa,
     wqkv, wout, wt, perm, sel, selt, normal, inv,
     normw, cotw, nmt, vt, dmt, mixt, mixp, dqkvt, r_q, r_o,
-    oa, ot, core_s, core_r,
+    oa, ot, core_s, core_r, own,
     a1, ra1, a2, ra2, a3, ra3, b1, rb1, b2, rb2, b3, rb3, c1, rc1, c2, rc2, c3, rc3,
     dbias, bc, bx, by, bz,
     lsem, hs, hr, os, orr, cs, cr, xs, xr, ys, yr, zs, zr,
@@ -281,16 +281,18 @@
     core_copies = []
     for y in range(NY):
         core_s[y] = grad_block(0, y).astype(BF)
-        if y % 2 == 1:
-            pair, k = slice(y - 1, y + 1), 1 + y // 2
-            core_copies.append(send(core_s.at[pair], core_r.at[pair], cs.at[k], cr.at[k], at_core()))
-
+        if y % 4 == 3:
+            group, k = slice(y - 3, y + 1), 1 + y // 4
+            core_copies.append(send(core_s.at[group], core_r.at[group], cs.at[k], cr.at[k], at_core()))
+
+    for y in range(NY):
+        own[y] = grad_block(256, y)
     lane_low = iota((64, 128), 1) < 64
     kept = []
     for y in range(NY):
-        if y % 2 == 0:
-            core_copies[y // 2].wait()
-        total = grad_block(256, y) + core_r[y].astype(F32)
+        if y % 4 == 0:
+            core_copies[y // 4].wait()
+        total = own[y] + core_r[y].astype(F32)
         for x in range(NX):
             a1[x, y] = total[32 * x : 32 * x + 32].astype(BF)
         b1[y] = total[128:192].astype(BF)
@@ -469,7 +471,7 @@
             V((2, D, WIN), BF), V((2, D, WIN), BF), V((2, 3 * D, WIN), BF),
             V((2, 4 * D, WIN), BF), V((2, 4 * D, WIN), BF),
             V((3, 3, 6, 4, D), BF), V((3, 3, 6, 4, D), BF),
-            V((NY, 256, 256), BF), V((NY, 256, 256), BF),
+            V((NY, 256, 256), BF), V((NY, 256, 256), BF), V((NY, 256, 256), F32),
             V((NX, NY, 32, 256), BF), V((3, NY, 32, 256), BF),
             V((NY, 32, 256), BF), V((7, 32, 256), BF),
             V((4, 16, 128), F32), V((7, 16, 128), F32),

time: 62.6 us -> 61.7 us (0.986)
  Pallas kernels: 60.7 us -> 59.9 us
    pallas_call x1, Pallas kernels: 58.9 us -> 58 us  [shards(): pl.pallas_call(kernel, out_shape=[jax.ShapeDtypeStruct((6, 12, 4, D), BF)...]
where the time goes in v5:
time: 61.7 us; the launch traced here: 60.6 us
  Pallas kernels  59.9 us (97%)
  between operations  0.64 us (1%)
    pallas_call x1, Pallas kernels, shards(): pl.pallas_call(kernel, out_shape=[jax.ShapeDtypeStruct((6, 12, 4, D), BF)...  58 us
    pallas_call x1, Pallas kernels, shards(): pl.pallas_call(place, out_shape=[jax.ShapeDtypeStruct(x.shape, x.dtype) f...  1.87 us

profile of v5, /device:TPU:6, one launch (start us, length us, event | category | flops | bytes accessed | tf_op | source)
XLA Modules:
  0.0 60.6 jit_solution(17063392860855925824)
XLA Ops:
  0.6 58.0 %swin_block.1 = (bf16[6,12,4,512]{3,2,1,0:T(4,128)(2,1)}, bf16[6,12,4,512]{3,2,1,0:T(4,128)(2,1)}, f32[32,48]{1,0:T(8,128)}, f32[16,32]{1,0:T(8,128)}, f32[1,8]{1,0:T(1,128)}) custom-call(bf16[6,12,4,512]{3,2,1,0:T(4,128)(2,1)} %bitcast.6, bf16[6,12,4,512]{3,2,1,0:T(4,128)(2,1)} %bitcast.7, bf16[512,1536]{1,0:T(8,128)(2,1)} %wqkv_h.1, ...), custom_call_target="tpu_custom_call" | custom-call | tf_op jit(solution)/shard_map/swin_block/pallas_call | solution.py:449
  58.7 1.9 %place.1 = (bf16[6,12,4,512]{3,2,1,0:T(4,128)(2,1)}, bf16[6,12,4,512]{3,2,1,0:T(4,128)(2,1)}, f32[32,48]{1,0:T(8,128)}, f32[16,32]{1,0:T(8,128)}, f32[1,8]{1,0:T(1,128)}) custom-call(bf16[6,12,4,512]{3,2,1,0:T(4,128)(2,1)} %get-tuple-element.15.refs_0_, bf16[6,12,4,512]{3,2,1,0:T(4,128)(2,1)} %get-tuple-element.16.refs_1_, ...), custom_call_target="tpu_custom_call" | custom-call | tf_op jit(solution)/shard_map/place/pallas_call | solution.py:496
